TPU v7x, 32 devices: a whole 2x2x4 slice. The times are simulated.
32 devices in a mesh: ens: 2 (over x), space: 4 (over y, core), bin: 4 (over z).
Axes of the slice: x: 2, y: 2, z: 4, core: 2. Of those that a mesh axis runs over, the one named last changes fastest.
Arguments:
- spectrum: float32 [1296, 32768], P('bin', ('ens', 'space')), parts along dimension 1, may hold values from 0.05 to 1
- wind: float32 [2, 32768], P(None, ('ens', 'space')), parts along dimension 1, may hold values from -6 to 6
- sea_mask: int32 [16384], P('space'), may hold values 0 or 1
- neighbours: int32 [4, 16384], P(None, 'space'), may hold values from -4096 to 20479, as said below
- metric_x: float32 [16384], P('space'), may hold values from 0.05 to 0.3
- metric_y: float32 [16384], P('space'), may hold values from 0.05 to 0.3
- refraction: float32 [16384], P('space'), may hold values from -0.15 to 0.15
- freq_shift: float32 [16384], P('space'), may hold values from -0.15 to 0.15
- dia_bins: int32 [4, 1296], replicated, may hold values from 0 to 1295
- dia_wts: float32 [2, 1296], replicated, may hold values from 0 to 1
Outputs:
- spectrum_next: float32 [1296, 32768], P(None, ('ens', 'space', 'bin')), parts along dimension 1
There are 2 independent parts, one for each index of `ens`. A program takes and returns all parts, laid end to end along the dimension named above; an argument that names none is the same for every part. Nothing has to cross between parts.
Inputs may be any that keep to these rules, and one draw needn't show every extreme that they name: `neighbours`: row 0 is p + 1 to p + 3 and row 1 is p - 3 to p - 1 for point p; row 2 is p + k and row 3 is p - k with k from 2048 to 4096. Indices outside 0 to 16383 mean open boundary.
All inputs are finite; a program needn't handle non-finite values. No bound on the sum of `sea_mask` on one device may be relied on, other than what follows from the above.
Results may differ from a plain program's by a relative error of at most 0.0003.
Values sent between devices are 32-bit elements; how exact they have to be, the bound alone decides.
No kernel may reach another device: no remote copies, remote signals or barrier semaphores. Data moves between devices by JAX's collectives and lax.ppermute only.
A program may use at most 192 MiB of HBM per device.

v0:
```python
import functools
import itertools

import jax
import jax.numpy as jnp
import numpy as np
from jax import lax
from jax.experimental import pallas as pl
from jax.experimental.pallas import tpu as pltpu
from jax.sharding import PartitionSpec as P

ND = 36


def extended(array, sides, width):
    for axis, dim in sides:
        peers, length = (lax.axis_size(axis), array.shape[dim])
        up = [(i, (i + 1) % peers) for i in range(peers - 1)]
        down = [(j, i) for i, j in up]
        last = lax.slice_in_dim(array, length - width, length, axis=dim)
        initial = lax.slice_in_dim(array, 0, width, axis=dim)
        before = lax.ppermute(last, axis, up)
        after = lax.ppermute(initial, axis, down)
        array = jnp.concatenate([before, array, after], axis=dim)
    return array


def bin_tables(index, nfreq, ndir):
    freq = (index // ndir).astype(jnp.float32)
    direc = index % ndir
    fratio = jnp.exp(jnp.log(1.1) * (freq - (nfreq - 1)))
    speed = jnp.exp(-jnp.log(1.1) * freq)
    theta = 2.0 * jnp.pi * (direc.astype(jnp.float32) + 0.5) / ndir
    return (fratio, speed, jnp.cos(theta), jnp.sin(theta), direc == 0, direc == ndir - 1)


def spatial_term(wet, padded, local, metric_x, metric_y, speed, cosv, sinv):
    east = jnp.take(padded, local[0], axis=1)
    west = jnp.take(padded, local[1], axis=1)
    north = jnp.take(padded, local[2], axis=1)
    south = jnp.take(padded, local[3], axis=1)
    along_x = metric_x[None, :] * (speed * cosv)[:, None]
    along_y = metric_y[None, :] * (speed * sinv)[:, None]
    flux_x = jnp.abs(along_x) * (wet - jnp.where(along_x > 0, west, east))
    flux_y = jnp.abs(along_y) * (wet - jnp.where(along_y > 0, south, north))
    return flux_x + flux_y


def spectral_term(wet, padded, ndir, first, last, refraction, freq_shift, speed, cosv):
    rows = wet.shape[0]

    def moved_rows(offset):
        return lax.slice_in_dim(padded, ndir + offset, ndir + offset + rows, axis=0)

    prev_dir = jnp.where(first[:, None], moved_rows(ndir - 1), moved_rows(-1))
    next_dir = jnp.where(last[:, None], moved_rows(1 - ndir), moved_rows(1))
    lower = moved_rows(-ndir)
    upper = moved_rows(ndir)
    turning = refraction[None, :] * cosv[:, None]
    shifting = freq_shift[None, :] * speed[:, None]
    flux_t = jnp.abs(turning) * (wet - jnp.where(turning > 0, prev_dir, next_dir))
    flux_s = jnp.abs(shifting) * (wet - jnp.where(shifting > 0, lower, upper))
    return flux_t + flux_s


def source_step(
    moved, wind, maskf, fratio, speed, cosv, sinv, plus_fwd, minus_fwd, plus_back, minus_back
):
    steep = jnp.mean(moved * (fratio * fratio)[:, None], axis=0)
    drive = jnp.maximum(
        0.0,
        wind[0][None, :] * cosv[:, None] + wind[1][None, :] * sinv[:, None] - 0.5 * speed[:, None],
    )
    s_in = 0.3 * drive * drive * moved
    s_ds = -6.0 * fratio[:, None] * steep[None, :] * moved
    e_plus = plus_fwd(moved)
    e_minus = minus_fwd(moved)
    delta = (
        8.0
        * (fratio**4)[:, None]
        * (
            moved * moved * (e_plus / 1.25**4 + e_minus / 0.75**4)
            - 2.0 * moved * e_plus * e_minus / 0.9375**4
        )
    )
    s_nl = -2.0 * delta + plus_back(delta) + minus_back(delta)
    return (moved + 0.5 * (s_in + s_ds + s_nl)) * maskf[None, :]


def pair_matrix(first_bins, second_bins, weight, count):
    columns = jnp.arange(count, dtype=jnp.int32)[None, :]
    return weight[:, None] * (first_bins[:, None] == columns).astype(jnp.float32) + (1.0 - weight)[
        :, None
    ] * (second_bins[:, None] == columns).astype(jnp.float32)


def forward_product(matrix, values):
    return jnp.dot(
        matrix, values, precision=lax.Precision.HIGHEST, preferred_element_type=jnp.float32
    )


def backward_product(matrix, values):
    return lax.dot_general(
        matrix,
        values,
        (((0,), (0,)), ((), ())),
        precision=lax.Precision.HIGHEST,
        preferred_element_type=jnp.float32,
    )


def on_device(
    spectrum,
    wind,
    sea_mask,
    neighbours,
    metric_x,
    metric_y,
    refraction,
    freq_shift,
    dia_bins,
    dia_wts,
):
    bins_dev, points_dev = spectrum.shape
    nbins = dia_bins.shape[1]
    ndir = ND
    nfreq = nbins // ndir
    space_pos = lax.axis_index("space")
    bin_pos = lax.axis_index("bin")
    maskf = sea_mask.astype(jnp.float32)
    wet = spectrum * maskf[None, :]
    padded = extended(wet, (("space", 1),), points_dev)
    base = space_pos * points_dev - points_dev
    local = neighbours - base
    own_bins = bin_pos * bins_dev + jnp.arange(bins_dev, dtype=jnp.int32)
    fratio, speed, cosv, sinv, first, last = bin_tables(own_bins, nfreq, ndir)
    spatial = spatial_term(wet, padded, local, metric_x, metric_y, speed, cosv, sinv)
    share = points_dev // lax.axis_size("bin")
    start = bin_pos * share
    all_bins = jnp.arange(nbins, dtype=jnp.int32)
    fratio_all, speed_all, cos_all, sin_all, first_all, last_all = bin_tables(all_bins, nfreq, ndir)
    bin_pad = extended(wet, (("bin", 0),), ndir)
    spectral = spectral_term(wet, bin_pad, ndir, first, last, refraction, freq_shift, speed, cosv)
    moved_own = wet - spatial - spectral
    moved = lax.all_to_all(moved_own, "bin", split_axis=1, concat_axis=0, tiled=True)
    wind_part = lax.dynamic_slice_in_dim(wind, start, share, 1)
    mask_part = lax.dynamic_slice_in_dim(maskf, start, share, 0)
    plus_matrix = pair_matrix(dia_bins[0], dia_bins[1], dia_wts[0], nbins)
    minus_matrix = pair_matrix(dia_bins[2], dia_bins[3], dia_wts[1], nbins)
    result = source_step(
        moved,
        wind_part,
        mask_part,
        fratio_all,
        speed_all,
        cos_all,
        sin_all,
        lambda v: forward_product(plus_matrix, v),
        lambda v: forward_product(minus_matrix, v),
        lambda v: backward_product(plus_matrix, v),
        lambda v: backward_product(minus_matrix, v),
    )
    return result


LANES = 128
ROWS = 8
EDGE = 16
QUART = ND // 4
PIECES = 3
VMEM_ASK = 60 << 20
GROUP = 4


def chunk_plan(nloc):
    mid = nloc // 2
    plan = [(mid - d, 2 * d, 2) for d in range(1, mid + 1)]
    if mid > 3:
        plan[2] = (mid - 3, 3, 3)
    else:
        plan.insert(0, (mid, 1, 1))
    return plan


def freqs_of(chunk):
    first, step, count = chunk
    return [first + i * step for i in range(count)]


def halo_groups(plan):
    return [g for g in (plan[:1], plan[1:]) if g]


def slots_of(group):
    return {f: i for i, f in enumerate(f for chunk in group for f in freqs_of(chunk))}


def runs_of(freqs):
    runs = []
    for f in sorted(freqs):
        if runs and runs[-1][1] == f:
            runs[-1] = (runs[-1][0], f + 1)
        else:
            runs.append((f, f + 1))
    return runs


def prep_kernel(points, bins, blocks, groups, full, spec_hbm, mask_ref, *refs):
    ngr = len(groups)
    nloc = bins // ND
    hs_hbm, hn_hbm = refs[:ngr], refs[ngr : 2 * ngr]
    if full:
        wet_hbm, low_hbm, high_hbm = refs[2 * ngr : 2 * ngr + 3]
    spec_v, wet_v, edge_v, in_sem, out_sem = refs[-5:]
    tiles = points // LANES
    half = ND // 2
    where = {f: (i, k) for i, group in enumerate(groups) for f, k in slots_of(group).items()}
    loads = []
    spans = []
    for lo, hi in blocks:
        start = lo * ND // ROWS * ROWS
        stop = min(-(-hi * ND // ROWS) * ROWS, bins)
        spans.append((start, stop))
        rows = pl.ds(start, stop - start)
        copy = pltpu.make_async_copy(spec_hbm.at[rows], spec_v.at[rows], in_sem.at[len(loads)])
        copy.start()
        loads.append(copy)
    masks = [mask_ref[:, c * LANES : (c + 1) * LANES].astype(jnp.float32) for c in range(tiles)]
    copies = []

    def send(src, dst):
        copy = pltpu.make_async_copy(src, dst, out_sem.at[len(copies)])
        copy.start()
        copies.append(copy)

    for (lo, hi), (start, stop), load in zip(blocks, spans, loads):
        load.wait()

        def turn(g0, count):
            for c0 in range(0, tiles, ROWS):
                cols = range(c0, c0 + ROWS)
                block = jnp.stack(
                    [spec_v[pl.ds(g0, count), c * LANES : (c + 1) * LANES] * masks[c] for c in cols], axis=0
                )
                block = jnp.swapaxes(block, 0, 1)
                for i in range(count):
                    wet_v[pl.ds(pl.multiple_of((g0 + i) * tiles + c0, ROWS), ROWS), :] = block[i]

        def relayout(t, _):
            turn(pl.multiple_of(start + t * ROWS, ROWS), ROWS)
            return 0

        lax.fori_loop(0, (stop - start) // ROWS, relayout, 0)
        rest = (stop - start) % ROWS
        if rest:
            g0 = stop - rest
            for c in range(tiles):
                tile = spec_v[pl.ds(g0, rest), c * LANES : (c + 1) * LANES]
                wet_v[pl.ds(g0 * tiles + c, rest, stride=tiles), :] = tile * masks[c]
        for f in range(lo, hi):
            base = f * ND * tiles
            if f in where:
                i, k = where[f]
                for side, (j0, row) in enumerate(((3 * QUART, tiles - 1), (QUART, 0))):
                    at = base + j0 * tiles + row
                    edge_v[f, side, ROWS:EDGE, :] = jnp.zeros((EDGE - ROWS, LANES), jnp.float32)
                    edge_v[f, side, 0:ROWS, :] = wet_v[pl.ds(at, ROWS, stride=tiles), :]
                    edge_v[f, side, ROWS : ROWS + 1, :] = wet_v[pl.ds(at + ROWS * tiles, 1), :]
                span = half * tiles
                send(wet_v.at[pl.ds(base, span)], hs_hbm[i].at[k, pl.ds(0, span)])
                send(wet_v.at[pl.ds(base + span, span)], hn_hbm[i].at[k, pl.ds(0, span)])
                send(edge_v.at[f, 0], hs_hbm[i].at[k, pl.ds(span, EDGE)])
                send(edge_v.at[f, 1], hn_hbm[i].at[k, pl.ds(span, EDGE)])
            if full:
                own = pl.ds(base, ND * tiles)
                if f == nloc - 1:
                    send(wet_v.at[own], low_hbm)
                if f == 0:
                    send(wet_v.at[own], high_hbm)
                send(wet_v.at[own], wet_hbm.at[own])
    for copy in copies:
        copy.wait()


def prep(spectrum, mask, blocks, groups, full):
    bins, points = spectrum.shape
    nloc = bins // ND
    tiles = points // LANES
    halo_rows = ND // 2 * tiles + EDGE
    halos = [jax.ShapeDtypeStruct((len(slots_of(g)), halo_rows, LANES), jnp.float32) for g in groups]
    one = jax.ShapeDtypeStruct((ND * tiles, LANES), jnp.float32)
    outs = halos + halos
    if full:
        outs += [jax.ShapeDtypeStruct((bins * tiles, LANES), jnp.float32), one, one]
    anywhere = pl.BlockSpec(memory_space=pl.ANY)
    count = sum(hi - lo for lo, hi in blocks)
    sends = 4 * sum(len(slots_of(g)) for g in groups) + (nloc + 2 if full else 0)
    res = pl.pallas_call(
        functools.partial(prep_kernel, points, bins, blocks, groups, full),
        out_shape=outs,
        in_specs=[anywhere, pl.BlockSpec(memory_space=pltpu.VMEM)],
        out_specs=[anywhere] * len(outs),
        scratch_shapes=[
            pltpu.VMEM((bins, points), jnp.float32),
            pltpu.VMEM((bins * tiles, LANES), jnp.float32),
            pltpu.VMEM((nloc, 2, EDGE, LANES), jnp.float32),
            pltpu.SemaphoreType.DMA((len(blocks),)),
            pltpu.SemaphoreType.DMA((sends,)),
        ],
        compiler_params=pltpu.CompilerParams(vmem_limit_bytes=VMEM_ASK),
        cost_estimate=pl.CostEstimate(flops=0, bytes_accessed=count * 3_000_000, transcendentals=0),
        name="prep",
    )(spectrum, mask)
    ngr = len(groups)
    return res[:ngr], res[ngr : 2 * ngr], res[2 * ngr :]


def front_kernel(
    tiles, shares, kmin, kmax, chunk, edge, tab_ref, dir_ref, pos_ref, nbr_ref, par_ref, hs_ref, hn_ref, wet_ref, *refs
):
    near, outs, ext_ref = refs[: -shares - 1], refs[-shares - 1 : -1], refs[-1]
    place = pl.program_id(0)
    speed = tab_ref[chunk[0] + chunk[1] * place]
    first = place == 0
    half = ND // 2
    span = half * tiles
    south, north = tiles, ROWS
    pitch = 2 * (2 * tiles + ROWS)

    def rows_at(j, row, count=ROWS):
        return pl.ds(j * pitch + 2 * row, count, stride=2)

    def extend(q, _):
        for t in range(0, tiles, ROWS):
            ext_ref[rows_at(q, t), :] = hs_ref[0, pl.ds(pl.multiple_of(q * tiles + t, ROWS), ROWS), :]
            ext_ref[rows_at(q, south + t), :] = wet_ref[0, q, t : t + ROWS, :]
            ext_ref[rows_at(half + q, north + t), :] = wet_ref[0, half + q, t : t + ROWS, :]
            ext_ref[rows_at(half + q, north + tiles + t), :] = hn_ref[
                0, pl.ds(pl.multiple_of(q * tiles + t, ROWS), ROWS), :
            ]
        return 0

    lax.fori_loop(0, half, extend, 0, unroll=2)
    for q in range(QUART):
        ext_ref[pl.ds((QUART + q) * pitch + 2 * (south + tiles), 1), :] = hn_ref[0, span + q : span + q + 1, :]
        ext_ref[pl.ds((3 * QUART + q) * pitch + 2 * (north - 1), 1), :] = hs_ref[0, span + q : span + q + 1, :]

    side = jnp.where(first, 1.0, -1.0)
    per_share = tiles // shares
    steps = [(d, k) for d in range(shares) for k in range(per_share // ROWS)]
    firsts = {}
    for d, k in steps:
        share = lax.rem(pos_ref[0] + d, shares)
        firsts[d, k] = pl.multiple_of(share * per_share + k * ROWS, ROWS)
    sub = lax.broadcasted_iota(jnp.int32, (ROWS, LANES), 0)
    lanes, rels = {}, {}
    for way in range(4):
        for step in steps:
            src = nbr_ref[way, pl.ds(firsts[step], ROWS), :]
            lanes[way, step] = src & (LANES - 1)
            rels[way, step] = (src >> 7) - (sub + firsts[step])

    def picked(j, own, step, way, offsets):
        out = None
        for r in offsets:
            window = ext_ref[rows_at(j, own + firsts[step] + r), :]
            got = jnp.take_along_axis(window, lanes[way, step], axis=1, mode="promise_in_bounds")
            out = got if out is None else jnp.where(rels[way, step] == r, got, out)
        return out

    for quad in range(4):
        cos_up = quad in (0, 3)
        own, way_y, off_y = (
            (south, 3, range(-(kmax // LANES), -(kmin // LANES) + 1))
            if quad < 2
            else (north, 2, range(kmin // LANES, kmax // LANES + 1))
        )
        way_x, off_x = (1, (-1, 0)) if cos_up else (0, (0, 1))

        def body(q, _):
            j = quad * QUART + q
            jprev = jnp.where(j == 0, ND - 1, j - 1)
            jnext = jnp.where(j == ND - 1, 0, j + 1)
            acos = jnp.abs(dir_ref[0, j])
            asin = jnp.abs(dir_ref[1, j])
            ax, ay = speed * acos, speed * asin
            for step in steps:
                at = pl.ds(firsts[step], ROWS)
                wet = wet_ref[0, j, at, :]
                e_y = picked(j, own, step, way_y, off_y)
                e_x = picked(j, own, step, way_x, off_x)
                rf, fs = par_ref[2, at, :], par_ref[3, at, :]
                e_prev, e_next = wet_ref[0, jprev, at, :], wet_ref[0, jnext, at, :]
                e_t = jnp.where(rf > 0, e_prev, e_next) if cos_up else jnp.where(rf < 0, e_prev, e_next)
                if edge:
                    inner, low, high = (ref[0, j, at, :] for ref in near)
                    outer = jnp.where(first, low, high)
                    e_s = jnp.where(fs * side > 0, outer, inner)
                else:
                    e_s = jnp.where(fs > 0, near[0][0, j, at, :], near[1][0, j, at, :])
                spatial = (par_ref[0, at, :] * ax) * (wet - e_x) + (par_ref[1, at, :] * ay) * (wet - e_y)
                spectral = (jnp.abs(rf) * acos) * (wet - e_t) + (jnp.abs(fs) * speed) * (wet - e_s)
                d, k = step
                outs[d][j, k * ROWS : (k + 1) * ROWS, :] = wet - spatial - spectral
            return 0

        lax.fori_loop(0, QUART, body, 0)


def front(speed, dirs, pos, nbr, par, hs, hn, slot, wet, ends, chunk, shares, kmin, kmax):
    first, step, count = chunk
    tiles = nbr.shape[1]
    nloc = wet.shape[0]
    smem = pl.BlockSpec(memory_space=pltpu.SMEM)

    def freq_spec(start, step):
        return pl.BlockSpec((1, ND, tiles, LANES), lambda i: (start + i * step, 0, 0, 0))

    halo_spec = pl.BlockSpec((1,) + hs.shape[1:], lambda i: (slot + i, 0, 0))

    def whole(shape):
        return pl.BlockSpec(shape, lambda i: (0,) * len(shape))

    if ends:
        near, near_specs = (wet,) + ends, [freq_spec(1, nloc - 3), freq_spec(0, 0), freq_spec(0, 0)]
    else:
        near, near_specs = (wet, wet), [freq_spec(first - 1, step), freq_spec(first + 1, step)]
    rows = tiles // shares
    return pl.pallas_call(
        functools.partial(front_kernel, tiles, shares, kmin, kmax, chunk, bool(ends)),
        grid=(count,),
        out_shape=[jax.ShapeDtypeStruct((count * ND, rows, LANES), jnp.float32)] * shares,
        in_specs=[smem] * 3
        + [whole(nbr.shape), whole(par.shape), halo_spec, halo_spec, freq_spec(first, step)]
        + near_specs,
        out_specs=[pl.BlockSpec((ND, rows, LANES), lambda i: (i, 0, 0))] * shares,
        scratch_shapes=[pltpu.VMEM((ND * 2 * (2 * tiles + ROWS), LANES), jnp.float32)],
        compiler_params=pltpu.CompilerParams(vmem_limit_bytes=VMEM_ASK),
        cost_estimate=pl.CostEstimate(flops=0, bytes_accessed=count * 22_000_000, transcendentals=0),
        name="front",
    )(speed, dirs, pos, nbr, par, hs, hn, wet, *near)


def tail_kernel(nfreq, bins_dev, plan, spot_ref, wts_ref, ftab_ref, frs_ref, dir_ref, pos_ref, wind_ref, mask_ref, *refs):
    out_hbm, mv, base, a0, a1, a2, a3, dw, out_v, in_sem, out_sem = refs[-11:]
    parts = refs[:-11]
    nparts = len(parts)
    shares = nparts // len(plan)
    nbins = nfreq * ND
    loads = []
    block = ND * ROWS
    for c, chunk in enumerate(plan):
        for d in range(shares):
            source = lax.rem(pos_ref[0] + (shares - d), shares)
            for i, f in enumerate(freqs_of(chunk)):
                rows = pl.ds(pl.multiple_of((source * bins_dev + f * ND) * ROWS, ROWS), block)
                part = parts[c * shares + d].at[pl.ds(i * block, block)]
                copy = pltpu.make_async_copy(part, mv.at[rows], in_sem.at[len(loads)])
                copy.start()
                loads.append(copy)
    zero = jnp.zeros((ROWS, LANES), jnp.float32)
    accs = (a0, a1, a2, a3)

    def tile(row):
        return pl.ds(pl.multiple_of(row, ROWS), ROWS)

    def clear(g, _):
        for acc in accs:
            acc[tile(g * ROWS), :] = zero
        return 0

    lax.fori_loop(0, nbins, clear, 0, unroll=8)
    for j in range(ND):
        dw[j] = wind_ref[0] * dir_ref[0, j] + wind_ref[1] * dir_ref[1, j]
    for copy in loads:
        copy.wait()

    def spread(g, shares_of):
        for i in range(GROUP):
            spots = [tile(spot_ref[4 * g + 4 * i + k]) for k in range(4)]
            old = [acc[at, :] for acc, at in zip(accs, spots)]
            for acc, at, was, add in zip(accs, spots, old, shares_of[4 * i : 4 * i + 4]):
                acc[at, :] = was + add

    def per_freq(f, carry):
        fr2, fr4, hspeed = ftab_ref[0, f], ftab_ref[1, f], ftab_ref[2, f]

        def per_group(t, carry):
            total, before = carry
            j0 = t * GROUP
            g0 = f * ND + j0
            own = [mv[tile((g0 + i) * ROWS), :] for i in range(GROUP)]
            found = [[mv[tile(spot_ref[4 * g0 + 4 * i + k]), :] for k in range(4)] for i in range(GROUP)]
            spread(jnp.maximum(g0 - GROUP, 0), before)
            shares_of = []
            for i in range(GROUP):
                m, (p0, p1, m0, m1) = own[i], found[i]
                wp, wm = wts_ref[2 * g0 + 2 * i], wts_ref[2 * g0 + 2 * i + 1]
                ep = p1 + wp * (p0 - p1)
                em = m1 + wm * (m0 - m1)
                mf = fr4 * m
                half = mf * (m * (ep * (1 / 1.25**4) + em * (1 / 0.75**4)) - ep * em * (2.0 / 0.9375**4))
                drive = jnp.maximum(0.0, dw[j0 + i] - hspeed)
                base[tile((g0 + i) * ROWS), :] = m + 0.15 * (drive * drive) * m - 2.0 * half
                sp, sm = wp * half, wm * half
                shares_of += [sp, half - sp, sm, half - sm]
                total = total + m
            return total, tuple(shares_of)

        steep, before = carry
        part, before = lax.fori_loop(0, ND // GROUP, per_group, (zero, before), unroll=3)
        return steep + part * fr2, before

    steep, before = lax.fori_loop(0, nfreq, per_freq, (zero, (zero,) * (4 * GROUP)))
    spread(nbins - GROUP, before)
    steep = steep * (1.0 / nbins)
    mask = mask_ref[...].astype(jnp.float32)
    per = nbins // PIECES
    copies = []
    for p in range(PIECES):

        def finish(t, _):
            g0 = t * ROWS
            done = []
            for i in range(ROWS):
                at = tile((g0 + i) * ROWS)
                mine = base[at, :] - (frs_ref[g0 + i] * steep) * mv[at, :]
                done.append((mine + ((a0[at, :] + a1[at, :]) + (a2[at, :] + a3[at, :]))) * mask)
            turned = jnp.swapaxes(jnp.stack(done, axis=0), 0, 1)
            for c in range(ROWS):
                out_v[pl.ds(pl.multiple_of(g0, ROWS), ROWS), c * LANES : (c + 1) * LANES] = turned[c]
            return 0

        lax.fori_loop(p * per // ROWS, (p + 1) * per // ROWS, finish, 0)
        rows = pl.ds(p * per, per)
        copy = pltpu.make_async_copy(out_v.at[rows], out_hbm.at[rows], out_sem.at[p])
        copy.start()
        copies.append(copy)
    for copy in copies:
        copy.wait()


def tail(parts, plan, bins_dev, dia_bins, dia_wts, ftab, frs, dirs, pos, wind, mask):
    nbins = dia_bins.shape[1]
    nfreq = nbins // ND
    anywhere = pl.BlockSpec(memory_space=pl.ANY)
    smem = pl.BlockSpec(memory_space=pltpu.SMEM)
    vmem = pl.BlockSpec(memory_space=pltpu.VMEM)
    points = ROWS * LANES
    spots = (dia_bins * ROWS).T.reshape(-1)
    wts = dia_wts.T.reshape(-1)
    field = pltpu.VMEM((nbins * ROWS, LANES), jnp.float32)
    return pl.pallas_call(
        functools.partial(tail_kernel, nfreq, bins_dev, plan),
        out_shape=jax.ShapeDtypeStruct((nbins, points), jnp.float32),
        in_specs=[smem] * 6 + [vmem] * 2 + [anywhere] * len(parts),
        out_specs=anywhere,
        scratch_shapes=[field] * 6
        + [
            pltpu.VMEM((ND, ROWS, LANES), jnp.float32),
            pltpu.VMEM((nbins, points), jnp.float32),
            pltpu.SemaphoreType.DMA((nbins // ND,)),
            pltpu.SemaphoreType.DMA((PIECES,)),
        ],
        compiler_params=pltpu.CompilerParams(vmem_limit_bytes=VMEM_ASK),
        cost_estimate=pl.CostEstimate(flops=0, bytes_accessed=70_000_000, transcendentals=0),
        name="tail",
    )(spots, wts, ftab, frs, dirs, pos, wind, mask, *parts)


def fast_on_device(
    spectrum, wind, sea_mask, neighbours, metric_x, metric_y, refraction, freq_shift, dia_bins, dia_wts
):
    bins_dev, points = spectrum.shape
    nbins = dia_bins.shape[1]
    nfreq = nbins // ND
    nloc = bins_dev // ND
    tiles = points // LANES
    shares = lax.axis_size("bin")
    share = points // shares
    bin_pos = lax.axis_index("bin")
    space_pos = lax.axis_index("space")
    plan = chunk_plan(nloc)

    freqs = np.arange(nfreq, dtype=np.float32)
    speed = jnp.asarray(np.exp(-np.log(1.1) * freqs.astype(np.float64)).astype(np.float32))
    ratio = np.exp(np.log(1.1) * (freqs.astype(np.float64) - (nfreq - 1)))
    ftab = jnp.asarray(
        np.stack([ratio**2, 4.0 * ratio**4, 0.5 * np.exp(-np.log(1.1) * freqs)]).astype(np.float32)
    )
    frs = jnp.asarray(np.repeat(3.0 * ratio, ND).astype(np.float32))
    theta = 2.0 * np.pi * (np.arange(ND) + 0.5) / ND
    dirs = jnp.asarray(np.stack([np.cos(theta), np.sin(theta)]).astype(np.float32))
    speed_own = lax.dynamic_slice_in_dim(speed, bin_pos * nloc, nloc, 0)

    groups = halo_groups(plan)
    early = runs_of(slots_of(groups[0]))
    mask_row = sea_mask.reshape(1, points)
    hs, hn, _ = prep(spectrum, mask_row, early, groups[:1], False)
    after, *_ = lax.optimization_barrier((spectrum, hs[0], hn[0]))
    whole_blocks = [(f, min(f + 2, nloc)) for f in range(0, nloc, 2)]
    hs_rest, hn_rest, (wet, low_out, high_out) = prep(after, mask_row, whole_blocks, groups[1:], True)
    wet = wet.reshape(nloc, ND, tiles, LANES)

    def line(array, axis, step):
        peers = lax.axis_size(axis)
        pairs = [(i, i + 1) for i in range(peers - 1)]
        if step < 0:
            pairs = [(b, a) for a, b in pairs]
        return lax.ppermute(array, axis, pairs)

    halos = []
    for south, north in zip(list(hs) + list(hs_rest), list(hn) + list(hn_rest)):
        if halos:
            south, north, *_ = lax.optimization_barrier((south, north) + halos[-1])
        halos.append((line(south, "space", 1), line(north, "space", -1)))
    low_in = line(low_out, "bin", 1).reshape(1, ND, tiles, LANES)
    high_in = line(high_out, "bin", -1).reshape(1, ND, tiles, LANES)

    nbr = (neighbours - space_pos * points).reshape(4, tiles, LANES)
    par = jnp.stack([metric_x, metric_y, refraction, freq_shift]).reshape(4, tiles, LANES)
    pos = bin_pos.reshape(1)
    kmin, kmax = points // 2, points
    parts = []
    order = pos
    for c, chunk in enumerate(plan):
        first, step, count = chunk
        gi, slot = [(i, slots_of(g)[first]) for i, g in enumerate(groups) if chunk in g][0]
        ends = (low_in, high_in) if first == 0 else None
        blocks = front(speed_own, dirs, order, nbr, par, *halos[gi], slot, wet, ends, chunk, shares, kmin, kmax)
        arrived = []
        for d, block in enumerate(blocks):
            rows = block.reshape(-1, LANES)
            if d and parts:
                rows, *_ = lax.optimization_barrier((rows,) + tuple(parts[-shares:][1:]))
            pairs = [(i, (i + d) % shares) for i in range(shares)]
            arrived.append(lax.ppermute(rows, "bin", pairs) if d else rows)
        earlier = tuple(parts[-shares:][1:]) if parts else (low_in, high_in) + sum(halos, ())
        order, *_ = lax.optimization_barrier((pos, blocks[0]) + earlier)
        parts += arrived
    wind_part = lax.dynamic_slice_in_dim(wind, bin_pos * share, share, 1).reshape(2, ROWS, LANES)
    mask_part = lax.dynamic_slice_in_dim(sea_mask, bin_pos * share, share, 0).reshape(ROWS, LANES)
    return tail(parts, plan, bins_dev, dia_bins, dia_wts, ftab, frs, dirs, pos, wind_part, mask_part)


def pick_path(spectrum, *others):
    bins_dev, points = spectrum.shape
    fits = bins_dev % (2 * ND) == ND and bins_dev > ND and points // lax.axis_size("bin") == ROWS * LANES
    return (fast_on_device if fits else on_device)(spectrum, *others)


def solution(mesh):
    return jax.shard_map(
        pick_path,
        mesh=mesh,
        in_specs=(
            P("bin", ("ens", "space")),
            P(None, ("ens", "space")),
            P("space"),
            P(None, "space"),
            P("space"),
            P("space"),
            P("space"),
            P("space"),
            P(),
            P(),
        ),
        out_specs=P(None, ("ens", "space", "bin")),
        check_vma=False,
    )
```

profile of v0, /device:TPU:1, one launch (start us, length us, event | category | flops | bytes accessed | tf_op | source)
XLA Modules:
  0.0 198.3 jit_solution(7679851374331510073)
XLA Ops:
  0.0 3.1 %prep.2 = (f32[2,592,128]{2,1,0:T(8,128)}, f32[2,592,128]{2,1,0:T(8,128)}) custom-call(f32[324,4096]{1,0:T(8,128)} %spec_hbm.2, s32[1,4096]{1,0:T(1,128)} %bitcast.59), custom_call_target="tpu_custom_call" | custom-call | bytes 6000000 | tf_op jit(solution)/shard_map/prep/pallas_call | solution.py:299
  3.1 4.5 %collective-permute-start = (f32[2,592,128]{2,1,0:T(8,128)}, f32[2,592,128]{2,1,0:T(8,128)S(1)}, u32[]{:S(2)}, u32[]{:S(2)}) collective-permute-start(f32[2,592,128]{2,1,0:T(8,128)} %get-tuple-element.43), channel_id=1, source_target_pairs={{0,4},{4,8},{8,12},{1,5},{5,9},{9,13},{2,6},{6,10},{10,14},{3,7},{... | collective-permute-start | bytes 1818632 | tf_op jit(solution)/shard_map/ppermute | solution.py:611
  7.7 0.0 copy-start.16
  7.7 0.0 copy-start.23
  7.7 0.0 copy-start.18
  7.7 0.0 copy-start.19
  7.7 0.0 copy-start.20
  7.7 0.0 copy-start.21
  7.8 2.1 %collective-permute-start.1 = (f32[2,592,128]{2,1,0:T(8,128)}, f32[2,592,128]{2,1,0:T(8,128)S(1)}, u32[]{:S(2)}, u32[]{:S(2)}) collective-permute-start(f32[2,592,128]{2,1,0:T(8,128)} %get-tuple-element.44), channel_id=1, source_target_pairs={{4,0},{8,4},{12,8},{5,1},{9,5},{13,9},{6,2},{10,6},{14,10},{7,3},{... | collective-permute-start | bytes 1818632 | tf_op jit(solution)/shard_map/ppermute | solution.py:611
  9.8 6.8 %prep.3 = (f32[7,592,128]{2,1,0:T(8,128)}, f32[7,592,128]{2,1,0:T(8,128)}, f32[10368,128]{1,0:T(8,128)}, f32[1152,128]{1,0:T(8,128)}, f32[1152,128]{1,0:T(8,128)}) custom-call(f32[324,4096]{1,0:T(8,128)} %spec_hbm.2, s32[1,4096]{1,0:T(1,128)} %bitcast.60), custom_call_target="tpu_custom_call" | custom-call | bytes 27000000 | tf_op jit(solution)/shard_map/prep/pallas_call | solution.py:299
  16.6 0.0 collective-permute-done.hs_ref
  16.6 2.9 %collective-permute-done.1.hn_ref = f32[2,592,128]{2,1,0:T(8,128)S(1)} collective-permute-done((f32[2,592,128]{2,1,0:T(8,128)}, f32[2,592,128]{2,1,0:T(8,128)S(1)}, u32[]{:S(2)}, u32[]{:S(2)}) %collective-permute-start.1) | collective-permute-done | bytes 606240 | tf_op jit(solution)/shard_map/ppermute | solution.py:611
  19.5 1.9 collective-permute-start.7
  21.4 2.5 %collective-permute-start.8 = (f32[7,592,128]{2,1,0:T(8,128)}, f32[7,592,128]{2,1,0:T(8,128)}, u32[]{:S(2)}, u32[]{:S(2)}) collective-permute-start(f32[7,592,128]{2,1,0:T(8,128)} %get-tuple-element.56), channel_id=1, source_target_pairs={{4,0},{8,4},{12,8},{5,1},{9,5},{13,9},{6,2},{10,6},{14,10},{7,3},{... | collective-permute-start | bytes 6365192 | tf_op jit(solution)/shard_map/ppermute | solution.py:611
  23.9 4.1 %collective-permute-start.5 = (f32[1152,128]{1,0:T(8,128)}, f32[1152,128]{1,0:T(8,128)}, u32[]{:S(2)}, u32[]{:S(2)}) collective-permute-start(f32[1152,128]{1,0:T(8,128)} %get-tuple-element.51), channel_id=1, source_target_pairs={{0,1},{1,2},{2,3},{4,5},{5,6},{6,7},{8,9},{9,10},{10,11},{12,13},{... | collective-permute-start | bytes 1769480 | tf_op jit(solution)/shard_map/ppermute | solution.py:611
  28.0 1.3 collective-permute-start.6
  29.3 0.6 copy.21
  30.0 0.6 dynamic_slice.11.tab_ref
  30.6 0.0 copy-done.19
  30.6 0.6 pad_maximum_fusion.par_ref
  31.2 0.0 copy-done.2
  31.2 16.3 %front.4 = (f32[72,8,128]{2,1,0:T(8,128)}, f32[72,8,128]{2,1,0:T(8,128)}, f32[72,8,128]{2,1,0:T(8,128)}, f32[72,8,128]{2,1,0:T(8,128)}) custom-call(f32[9]{0:T(128)} %dynamic_slice.11.tab_ref, f32[2,36]{1,0:T(2,128)} %constant.30.clone.dir_ref, s32[1]{0:T(128)} %bitcast.2.pos_ref, s32[4,32,128]{2,1,0:T(8,128)} %bitcast.51, ...), custom_call_target="tpu_custom_call" | custom-call | bytes 44000000 | tf_op jit(solution)/shard_map/front/pallas_call | solution.py:430
  47.5 2.1 %collective-permute-start.2 = (f32[576,128]{1,0:T(8,128)}, f32[576,128]{1,0:T(8,128)S(1)}, u32[]{:S(2)}, u32[]{:S(2)}) collective-permute-start(f32[576,128]{1,0:T(8,128)} %bitcast.75), channel_id=1, source_target_pairs={{0,1},{1,2},{2,3},{3,0},{4,5},{5,6},{6,7},{7,4},{8,9},{9,10},{10,1... | collective-permute-start | bytes 884744 | tf_op jit(solution)/shard_map/ppermute | solution.py:638
  49.6 0.0 collective-permute-done.5
  49.6 2.3 %collective-permute-start.3 = (f32[576,128]{1,0:T(8,128)}, f32[576,128]{1,0:T(8,128)S(1)}, u32[]{:S(2)}, u32[]{:S(2)}) collective-permute-start(f32[576,128]{1,0:T(8,128)} %bitcast.74), channel_id=1, source_target_pairs={{0,2},{1,3},{2,0},{3,1},{4,6},{5,7},{6,4},{7,5},{8,10},{9,11},{10,... | collective-permute-start | bytes 884744 | tf_op jit(solution)/shard_map/ppermute | solution.py:638
  51.9 0.0 collective-permute-done.6
  51.9 0.2 collective-permute-start.4
  52.2 0.0 collective-permute-done.7.hs_ref
  52.2 0.0 collective-permute-done.8.hn_ref
  52.2 1.3 copy-done.1
  53.5 16.3 %front.5 = (f32[72,8,128]{2,1,0:T(8,128)}, f32[72,8,128]{2,1,0:T(8,128)}, f32[72,8,128]{2,1,0:T(8,128)}, f32[72,8,128]{2,1,0:T(8,128)}) custom-call(f32[9]{0:T(128)} %dynamic_slice.11.tab_ref, f32[2,36]{1,0:T(2,128)} %constant.30.clone.dir_ref, s32[1]{0:T(128)} %bitcast.2.pos_ref, s32[4,32,128]{2,1,0:T(8,128)} %bitcast.52, ...), custom_call_target="tpu_custom_call" | custom-call | bytes 44000000 | tf_op jit(solution)/shard_map/front/pallas_call | solution.py:430
  69.8 0.0 collective-permute-done.2.refs_1_
  69.8 2.2 %collective-permute-done.3.refs_2_ = f32[576,128]{1,0:T(8,128)S(1)} collective-permute-done((f32[576,128]{1,0:T(8,128)}, f32[576,128]{1,0:T(8,128)S(1)}, u32[]{:S(2)}, u32[]{:S(2)}) %collective-permute-start.3) | collective-permute-done | bytes 294944 | tf_op jit(solution)/shard_map/ppermute | solution.py:638
  72.0 0.0 collective-permute-done.4.refs_3_
  72.1 6.6 %collective-permute-start.11 = (f32[576,128]{1,0:T(8,128)}, f32[576,128]{1,0:T(8,128)S(1)}, u32[]{:S(2)}, u32[]{:S(2)}) collective-permute-start(f32[576,128]{1,0:T(8,128)} %bitcast.78), channel_id=1, source_target_pairs={{0,3},{1,0},{2,1},{3,2},{4,7},{5,4},{6,5},{7,6},{8,11},{9,8},{10,9... | collective-permute-start | bytes 884744 | tf_op jit(solution)/shard_map/ppermute | solution.py:638
  78.6 1.2 collective-permute-start.10
  79.8 0.0 collective-permute-start.9
  79.8 23.0 %front.6 = (f32[108,8,128]{2,1,0:T(8,128)}, f32[108,8,128]{2,1,0:T(8,128)}, f32[108,8,128]{2,1,0:T(8,128)}, f32[108,8,128]{2,1,0:T(8,128)}) custom-call(f32[9]{0:T(128)} %dynamic_slice.11.tab_ref, f32[2,36]{1,0:T(2,128)} %constant.30.clone.dir_ref, s32[1]{0:T(128)} %bitcast.2.pos_ref, s32[4,32,128]{2,1,0:T(8,128)} %bitcast.53, ...), custom_call_target="tpu_custom_call" | custom-call | bytes 66000000 | tf_op jit(solution)/shard_map/front/pallas_call | solution.py:430
  102.9 0.0 collective-permute-done.11.refs_7_
  102.9 2.8 %collective-permute-done.10.refs_6_ = f32[576,128]{1,0:T(8,128)S(1)} collective-permute-done((f32[576,128]{1,0:T(8,128)}, f32[576,128]{1,0:T(8,128)S(1)}, u32[]{:S(2)}, u32[]{:S(2)}) %collective-permute-start.10) | collective-permute-done | bytes 294944 | tf_op jit(solution)/shard_map/ppermute | solution.py:638
  105.7 0.0 collective-permute-done.9.refs_5_
  105.7 0.6 collective-permute-start.14
  106.2 0.2 collective-permute-start.13
  106.4 1.5 collective-permute-start.12
  107.9 16.3 %front.7 = (f32[72,8,128]{2,1,0:T(8,128)}, f32[72,8,128]{2,1,0:T(8,128)}, f32[72,8,128]{2,1,0:T(8,128)}, f32[72,8,128]{2,1,0:T(8,128)}) custom-call(f32[9]{0:T(128)} %dynamic_slice.11.tab_ref, f32[2,36]{1,0:T(2,128)} %constant.30.clone.dir_ref, s32[1]{0:T(128)} %bitcast.2.pos_ref, s32[4,32,128]{2,1,0:T(8,128)} %bitcast.54, ...), custom_call_target="tpu_custom_call" | custom-call | bytes 44000000 | tf_op jit(solution)/shard_map/front/pallas_call | solution.py:430
  124.2 0.0 collective-permute-done.14.refs_11_
  124.3 20.2 %collective-permute-done.13.refs_10_ = f32[864,128]{1,0:T(8,128)S(1)} collective-permute-done((f32[864,128]{1,0:T(8,128)}, f32[864,128]{1,0:T(8,128)S(1)}, u32[]{:S(2)}, u32[]{:S(2)}) %collective-permute-start.13) | collective-permute-done | bytes 442400 | tf_op jit(solution)/shard_map/ppermute | solution.py:638
  144.5 0.0 collective-permute-done.12.refs_9_
  144.5 0.1 collective-permute-start.17
  144.5 3.4 %collective-permute-start.16 = (f32[576,128]{1,0:T(8,128)}, f32[576,128]{1,0:T(8,128)S(1)}, u32[]{:S(2)}, u32[]{:S(2)}) collective-permute-start(f32[576,128]{1,0:T(8,128)} %bitcast.71), channel_id=1, source_target_pairs={{0,2},{1,3},{2,0},{3,1},{4,6},{5,7},{6,4},{7,5},{8,10},{9,11},{10,... | collective-permute-start | bytes 884744 | tf_op jit(solution)/shard_map/ppermute | solution.py:638
  147.9 1.5 collective-permute-start.15
  149.4 0.6 copy.22
  150.0 0.3 copy.15
  150.3 0.9 reshape.87.spot_ref
  151.2 0.0 copy-done.22
  151.2 0.3 copy.16
  151.5 0.9 reshape.88.wts_ref
  152.4 1.3 dynamic-slice_bitcast_fusion.1.mask_ref
  153.7 0.0 collective-permute-done.17.refs_15_
  153.7 20.3 %collective-permute-done.16.refs_14_ = f32[576,128]{1,0:T(8,128)S(1)} collective-permute-done((f32[576,128]{1,0:T(8,128)}, f32[576,128]{1,0:T(8,128)S(1)}, u32[]{:S(2)}, u32[]{:S(2)}) %collective-permute-start.16) | collective-permute-done | bytes 294944 | tf_op jit(solution)/shard_map/ppermute | solution.py:638
  174.0 0.0 collective-permute-done.15.refs_13_
  174.1 0.7 copy-done.14
  174.8 0.1 copy-done.15
  174.9 23.4 %tail.1 = f32[1296,1024]{1,0:T(8,128)} custom-call(s32[5184]{0:T(1024)} %reshape.87.spot_ref, f32[2592]{0:T(1024)} %reshape.88.wts_ref, f32[3,36]{1,0:T(4,128)} %constant.28.clone.ftab_ref, f32[1296]{0:T(1024)} %constant.29.clone.frs_ref, f32[2,36]{1,0:T(2,128)} %constant.30.clone.dir_ref, s32[1]{0:T(128)} %bitcast.2.pos_ref, f32[2,8,128]{2,1,0:T(8,128)} %bitcast.61, ...), custom_call_target="tpu_custom_call" | custom-call | bytes 70000000 | tf_op jit(solution)/shard_map/tail/pallas_call | solution.py:554
  (39 shorter events, 0.1 us)
Async XLA Ops:
  0.0 149.4 %copy-start = (f32[2,4096]{1,0:T(2,128)S(1)}, f32[2,4096]{1,0:T(2,128)}, u32[]{:S(2)}) copy-start(f32[2,4096]{1,0:T(2,128)} %param.15) | copy-start | bytes 98308
  3.1 13.4 %collective-permute-start = (f32[2,592,128]{2,1,0:T(8,128)}, f32[2,592,128]{2,1,0:T(8,128)S(1)}, u32[]{:S(2)}, u32[]{:S(2)}) collective-permute-start(f32[2,592,128]{2,1,0:T(8,128)} %get-tuple-element.43), channel_id=1, source_target_pairs={{0,4},{4,8},{8,12},{1,5},{5,9},{9,13},{2,6},{6,10},{10,14},{3,7},{... | collective-permute-start | bytes 1818632 | tf_op jit(solution)/shard_map/ppermute | solution.py:611
  7.7 21.6 %copy-start.16 = (s32[4,4096]{1,0:T(4,128)S(1)}, s32[4,4096]{1,0:T(4,128)}, u32[]{:S(2)}) copy-start(s32[4,4096]{1,0:T(4,128)} %param.17) | copy-start | bytes 196612
  7.7 22.3 %copy-start.23 = (f32[36]{0:T(128)S(1)}, f32[36]{0:T(128)}, u32[]{:S(2)}) copy-start(f32[36]{0:T(128)} %constant.27.clone) | copy-start | bytes 436
  7.7 22.9 %copy-start.18 = (f32[4096]{0:T(1024)S(1)}, f32[4096]{0:T(1024)}, u32[]{:S(2)}) copy-start(f32[4096]{0:T(1024)} %param.21) | copy-start | bytes 49156
  7.7 22.9 %copy-start.19 = (f32[4096]{0:T(1024)S(1)}, f32[4096]{0:T(1024)}, u32[]{:S(2)}) copy-start(f32[4096]{0:T(1024)} %param.20) | copy-start | bytes 49156
  7.7 22.9 %copy-start.20 = (f32[4096]{0:T(1024)S(1)}, f32[4096]{0:T(1024)}, u32[]{:S(2)}) copy-start(f32[4096]{0:T(1024)} %param.19) | copy-start | bytes 49156
  7.7 22.9 %copy-start.21 = (f32[4096]{0:T(1024)S(1)}, f32[4096]{0:T(1024)}, u32[]{:S(2)}) copy-start(f32[4096]{0:T(1024)} %param.18) | copy-start | bytes 49156
  7.8 11.7 %collective-permute-start.1 = (f32[2,592,128]{2,1,0:T(8,128)}, f32[2,592,128]{2,1,0:T(8,128)S(1)}, u32[]{:S(2)}, u32[]{:S(2)}) collective-permute-start(f32[2,592,128]{2,1,0:T(8,128)} %get-tuple-element.44), channel_id=1, source_target_pairs={{4,0},{8,4},{12,8},{5,1},{9,5},{13,9},{6,2},{10,6},{14,10},{7,3},{... | collective-permute-start | bytes 1818632 | tf_op jit(solution)/shard_map/ppermute | solution.py:611
  16.6 14.7 %copy-start.2 = (f32[2,592,128]{2,1,0:T(8,128)}, f32[2,592,128]{2,1,0:T(8,128)S(1)}, u32[]{:S(2)}) copy-start(f32[2,592,128]{2,1,0:T(8,128)S(1)} %collective-permute-done.hs_ref) | copy-start | bytes 1818628
  19.5 11.8 %copy-start.3 = (f32[2,592,128]{2,1,0:T(8,128)}, f32[2,592,128]{2,1,0:T(8,128)S(1)}, u32[]{:S(2)}) copy-start(f32[2,592,128]{2,1,0:T(8,128)S(1)} %collective-permute-done.1.hn_ref) | copy-start | bytes 1818628
  19.5 32.7 %collective-permute-start.7 = (f32[7,592,128]{2,1,0:T(8,128)}, f32[7,592,128]{2,1,0:T(8,128)S(1)}, u32[]{:S(2)}, u32[]{:S(2)}) collective-permute-start(f32[7,592,128]{2,1,0:T(8,128)} %get-tuple-element.55), channel_id=1, source_target_pairs={{0,4},{4,8},{8,12},{1,5},{5,9},{9,13},{2,6},{6,10},{10,14},{3,7},{... | collective-permute-start | bytes 6365192 | tf_op jit(solution)/shard_map/ppermute | solution.py:611
  21.4 30.8 %collective-permute-start.8 = (f32[7,592,128]{2,1,0:T(8,128)}, f32[7,592,128]{2,1,0:T(8,128)}, u32[]{:S(2)}, u32[]{:S(2)}) collective-permute-start(f32[7,592,128]{2,1,0:T(8,128)} %get-tuple-element.56), channel_id=1, source_target_pairs={{4,0},{8,4},{12,8},{5,1},{9,5},{13,9},{6,2},{10,6},{14,10},{7,3},{... | collective-permute-start | bytes 6365192 | tf_op jit(solution)/shard_map/ppermute | solution.py:611
  23.9 25.7 %collective-permute-start.5 = (f32[1152,128]{1,0:T(8,128)}, f32[1152,128]{1,0:T(8,128)}, u32[]{:S(2)}, u32[]{:S(2)}) collective-permute-start(f32[1152,128]{1,0:T(8,128)} %get-tuple-element.51), channel_id=1, source_target_pairs={{0,1},{1,2},{2,3},{4,5},{5,6},{6,7},{8,9},{9,10},{10,11},{12,13},{... | collective-permute-start | bytes 1769480 | tf_op jit(solution)/shard_map/ppermute | solution.py:611
  28.0 23.9 %collective-permute-start.6 = (f32[1152,128]{1,0:T(8,128)}, f32[1152,128]{1,0:T(8,128)}, u32[]{:S(2)}, u32[]{:S(2)}) collective-permute-start(f32[1152,128]{1,0:T(8,128)} %get-tuple-element.52), channel_id=1, source_target_pairs={{1,0},{2,1},{3,2},{5,4},{6,5},{7,6},{9,8},{10,9},{11,10},{13,12},{... | collective-permute-start | bytes 1769480 | tf_op jit(solution)/shard_map/ppermute | solution.py:611
  47.5 22.3 %collective-permute-start.2 = (f32[576,128]{1,0:T(8,128)}, f32[576,128]{1,0:T(8,128)S(1)}, u32[]{:S(2)}, u32[]{:S(2)}) collective-permute-start(f32[576,128]{1,0:T(8,128)} %bitcast.75), channel_id=1, source_target_pairs={{0,1},{1,2},{2,3},{3,0},{4,5},{5,6},{6,7},{7,4},{8,9},{9,10},{10,1... | collective-permute-start | bytes 884744 | tf_op jit(solution)/shard_map/ppermute | solution.py:638
  49.6 22.4 %collective-permute-start.3 = (f32[576,128]{1,0:T(8,128)}, f32[576,128]{1,0:T(8,128)S(1)}, u32[]{:S(2)}, u32[]{:S(2)}) collective-permute-start(f32[576,128]{1,0:T(8,128)} %bitcast.74), channel_id=1, source_target_pairs={{0,2},{1,3},{2,0},{3,1},{4,6},{5,7},{6,4},{7,5},{8,10},{9,11},{10,... | collective-permute-start | bytes 884744 | tf_op jit(solution)/shard_map/ppermute | solution.py:638
  51.9 20.1 %collective-permute-start.4 = (f32[576,128]{1,0:T(8,128)}, f32[576,128]{1,0:T(8,128)S(1)}, u32[]{:S(2)}, u32[]{:S(2)}) collective-permute-start(f32[576,128]{1,0:T(8,128)} %bitcast.73), channel_id=1, source_target_pairs={{0,3},{1,0},{2,1},{3,2},{4,7},{5,4},{6,5},{7,6},{8,11},{9,8},{10,9... | collective-permute-start | bytes 884744 | tf_op jit(solution)/shard_map/ppermute | solution.py:638
  52.2 1.3 copy-start.1
  69.8 33.0 %copy-start.7 = (f32[576,128]{1,0:T(8,128)}, f32[576,128]{1,0:T(8,128)S(1)}, u32[]{:S(2)}) copy-start(f32[576,128]{1,0:T(8,128)S(1)} %collective-permute-done.2.refs_1_) | copy-start | bytes 884740
  72.0 30.8 %copy-start.8 = (f32[576,128]{1,0:T(8,128)}, f32[576,128]{1,0:T(8,128)S(1)}, u32[]{:S(2)}) copy-start(f32[576,128]{1,0:T(8,128)S(1)} %collective-permute-done.3.refs_2_) | copy-start | bytes 884740
  72.1 30.8 %copy-start.9 = (f32[576,128]{1,0:T(8,128)}, f32[576,128]{1,0:T(8,128)S(1)}, u32[]{:S(2)}) copy-start(f32[576,128]{1,0:T(8,128)S(1)} %collective-permute-done.4.refs_3_) | copy-start | bytes 884740
  72.1 30.8 %collective-permute-start.11 = (f32[576,128]{1,0:T(8,128)}, f32[576,128]{1,0:T(8,128)S(1)}, u32[]{:S(2)}, u32[]{:S(2)}) collective-permute-start(f32[576,128]{1,0:T(8,128)} %bitcast.78), channel_id=1, source_target_pairs={{0,3},{1,0},{2,1},{3,2},{4,7},{5,4},{6,5},{7,6},{8,11},{9,8},{10,9... | collective-permute-start | bytes 884744 | tf_op jit(solution)/shard_map/ppermute | solution.py:638
  78.6 27.0 %collective-permute-start.10 = (f32[576,128]{1,0:T(8,128)}, f32[576,128]{1,0:T(8,128)S(1)}, u32[]{:S(2)}, u32[]{:S(2)}) collective-permute-start(f32[576,128]{1,0:T(8,128)} %bitcast.77), channel_id=1, source_target_pairs={{0,2},{1,3},{2,0},{3,1},{4,6},{5,7},{6,4},{7,5},{8,10},{9,11},{10,... | collective-permute-start | bytes 884744 | tf_op jit(solution)/shard_map/ppermute | solution.py:638
  79.8 25.8 %collective-permute-start.9 = (f32[576,128]{1,0:T(8,128)}, f32[576,128]{1,0:T(8,128)S(1)}, u32[]{:S(2)}, u32[]{:S(2)}) collective-permute-start(f32[576,128]{1,0:T(8,128)} %bitcast.76), channel_id=1, source_target_pairs={{0,1},{1,2},{2,3},{3,0},{4,5},{5,6},{6,7},{7,4},{8,9},{9,10},{10,1... | collective-permute-start | bytes 884744 | tf_op jit(solution)/shard_map/ppermute | solution.py:638
  102.9 21.3 %copy-start.10 = (f32[576,128]{1,0:T(8,128)}, f32[576,128]{1,0:T(8,128)S(1)}, u32[]{:S(2)}) copy-start(f32[576,128]{1,0:T(8,128)S(1)} %collective-permute-done.11.refs_7_) | copy-start | bytes 884740
  105.7 18.6 %copy-start.11 = (f32[576,128]{1,0:T(8,128)}, f32[576,128]{1,0:T(8,128)S(1)}, u32[]{:S(2)}) copy-start(f32[576,128]{1,0:T(8,128)S(1)} %collective-permute-done.10.refs_6_) | copy-start | bytes 884740
  105.7 18.6 %copy-start.12 = (f32[576,128]{1,0:T(8,128)}, f32[576,128]{1,0:T(8,128)S(1)}, u32[]{:S(2)}) copy-start(f32[576,128]{1,0:T(8,128)S(1)} %collective-permute-done.9.refs_5_) | copy-start | bytes 884740
  105.7 18.6 %collective-permute-start.14 = (f32[864,128]{1,0:T(8,128)}, f32[864,128]{1,0:T(8,128)S(1)}, u32[]{:S(2)}, u32[]{:S(2)}) collective-permute-start(f32[864,128]{1,0:T(8,128)} %bitcast.69), channel_id=1, source_target_pairs={{0,3},{1,0},{2,1},{3,2},{4,7},{5,4},{6,5},{7,6},{8,11},{9,8},{10,9... | collective-permute-start | bytes 1327112 | tf_op jit(solution)/shard_map/ppermute | solution.py:638
  106.2 38.2 %collective-permute-start.13 = (f32[864,128]{1,0:T(8,128)}, f32[864,128]{1,0:T(8,128)S(1)}, u32[]{:S(2)}, u32[]{:S(2)}) collective-permute-start(f32[864,128]{1,0:T(8,128)} %bitcast.68), channel_id=1, source_target_pairs={{0,2},{1,3},{2,0},{3,1},{4,6},{5,7},{6,4},{7,5},{8,10},{9,11},{10,... | collective-permute-start | bytes 1327112 | tf_op jit(solution)/shard_map/ppermute | solution.py:638
  106.4 38.0 %collective-permute-start.12 = (f32[864,128]{1,0:T(8,128)}, f32[864,128]{1,0:T(8,128)S(1)}, u32[]{:S(2)}, u32[]{:S(2)}) collective-permute-start(f32[864,128]{1,0:T(8,128)} %bitcast.67), channel_id=1, source_target_pairs={{0,1},{1,2},{2,3},{3,0},{4,5},{5,6},{6,7},{7,4},{8,9},{9,10},{10,1... | collective-permute-start | bytes 1327112 | tf_op jit(solution)/shard_map/ppermute | solution.py:638
  107.9 41.5 %copy-start.17 = (s32[4,1296]{1,0:T(4,128)S(1)}, s32[4,1296]{1,0:T(4,128)}, u32[]{:S(2)}) copy-start(s32[4,1296]{1,0:T(4,128)} %param.22) | copy-start | bytes 62212
  107.9 43.3 %copy-start.22 = (f32[2,1296]{1,0:T(2,128)S(1)}, f32[2,1296]{1,0:T(2,128)}, u32[]{:S(2)}) copy-start(f32[2,1296]{1,0:T(2,128)} %param.23) | copy-start | bytes 31108
  124.2 49.8 %copy-start.4 = (f32[864,128]{1,0:T(8,128)}, f32[864,128]{1,0:T(8,128)S(1)}, u32[]{:S(2)}) copy-start(f32[864,128]{1,0:T(8,128)S(1)} %collective-permute-done.14.refs_11_) | copy-start | bytes 1327108
  144.5 29.6 %copy-start.5 = (f32[864,128]{1,0:T(8,128)}, f32[864,128]{1,0:T(8,128)S(1)}, u32[]{:S(2)}) copy-start(f32[864,128]{1,0:T(8,128)S(1)} %collective-permute-done.13.refs_10_) | copy-start | bytes 1327108
  144.5 29.6 %copy-start.6 = (f32[864,128]{1,0:T(8,128)}, f32[864,128]{1,0:T(8,128)S(1)}, u32[]{:S(2)}) copy-start(f32[864,128]{1,0:T(8,128)S(1)} %collective-permute-done.12.refs_9_) | copy-start | bytes 1327108
  144.5 9.3 %collective-permute-start.17 = (f32[576,128]{1,0:T(8,128)}, f32[576,128]{1,0:T(8,128)S(1)}, u32[]{:S(2)}, u32[]{:S(2)}) collective-permute-start(f32[576,128]{1,0:T(8,128)} %bitcast.72), channel_id=1, source_target_pairs={{0,3},{1,0},{2,1},{3,2},{4,7},{5,4},{6,5},{7,6},{8,11},{9,8},{10,9... | collective-permute-start | bytes 884744 | tf_op jit(solution)/shard_map/ppermute | solution.py:638
  144.5 29.5 %collective-permute-start.16 = (f32[576,128]{1,0:T(8,128)}, f32[576,128]{1,0:T(8,128)S(1)}, u32[]{:S(2)}, u32[]{:S(2)}) collective-permute-start(f32[576,128]{1,0:T(8,128)} %bitcast.71), channel_id=1, source_target_pairs={{0,2},{1,3},{2,0},{3,1},{4,6},{5,7},{6,4},{7,5},{8,10},{9,11},{10,... | collective-permute-start | bytes 884744 | tf_op jit(solution)/shard_map/ppermute | solution.py:638
  147.9 26.1 %collective-permute-start.15 = (f32[576,128]{1,0:T(8,128)}, f32[576,128]{1,0:T(8,128)S(1)}, u32[]{:S(2)}, u32[]{:S(2)}) collective-permute-start(f32[576,128]{1,0:T(8,128)} %bitcast.70), channel_id=1, source_target_pairs={{0,1},{1,2},{2,3},{3,0},{4,5},{5,6},{6,7},{7,4},{8,9},{9,10},{10,1... | collective-permute-start | bytes 884744 | tf_op jit(solution)/shard_map/ppermute | solution.py:638
  153.7 20.4 %copy-start.13 = (f32[576,128]{1,0:T(8,128)}, f32[576,128]{1,0:T(8,128)S(1)}, u32[]{:S(2)}) copy-start(f32[576,128]{1,0:T(8,128)S(1)} %collective-permute-done.17.refs_15_) | copy-start | bytes 884740
  174.0 0.7 copy-start.14
  174.0 0.9 copy-start.15
where the time goes:
time: 200 us; the launch traced here: 198 us
  Pallas kernels  105 us (52%)
  waiting for transfers between devices  48.4 us (24%)
  starting transfers between devices  36 us (18%)
  local copies, waits for them, and re-layouts  7.8 us (4%)
    pallas_call x4, Pallas kernels, front(): pl.pallas_call(functools.partial(front_kernel, tiles, shares, kmin, kmax,...  71.9 us
    ppermute x12, waiting for transfers between devices, fast_on_device(): arrived.append(lax.ppermute(rows, 'bin', pairs) if d else rows)  45.5 us
    pallas_call x1, Pallas kernels, tail(): pl.pallas_call(functools.partial(tail_kernel, nfreq, bins_dev, plan), out...  23.4 us
    ppermute x12, starting transfers between devices, fast_on_device(): arrived.append(lax.ppermute(rows, 'bin', pairs) if d else rows)  19.6 us
    ppermute x6, starting transfers between devices, line(): return lax.ppermute(array, axis, pairs)  16.4 us
    pallas_call x2, Pallas kernels, prep(): pl.pallas_call(functools.partial(prep_kernel, points, bins, blocks, group...  9.88 us
  transfers between devices with their start and end apart: 18, of which 5 were waited for; matrix products, arithmetic and copies ran while one was open for 3% of the time, Pallas kernels for 40%

commit v1 on v0

--- a/solution.py
+++ b/solution.py
@@ -168,7 +168,7 @@
 ROWS = 8
 EDGE = 16
 QUART = ND // 4
-PIECES = 3
+PIECES = 6
 VMEM_ASK = 60 << 20
 GROUP = 4
 
@@ -405,7 +405,7 @@
                 outs[d][j, k * ROWS : (k + 1) * ROWS, :] = wet - spatial - spectral
             return 0
 
-        lax.fori_loop(0, QUART, body, 0)
+        lax.fori_loop(0, QUART, body, 0, unroll=3)
 
 
 def front(speed, dirs, pos, nbr, par, hs, hn, slot, wet, ends, chunk, shares, kmin, kmax):
@@ -449,25 +449,21 @@
     shares = nparts // len(plan)
     nbins = nfreq * ND
     loads = []
-    block = ND * ROWS
     for c, chunk in enumerate(plan):
         for d in range(shares):
             source = lax.rem(pos_ref[0] + (shares - d), shares)
             for i, f in enumerate(freqs_of(chunk)):
-                rows = pl.ds(pl.multiple_of((source * bins_dev + f * ND) * ROWS, ROWS), block)
-                part = parts[c * shares + d].at[pl.ds(i * block, block)]
+                rows = pl.ds(source * bins_dev + f * ND, ND)
+                part = parts[c * shares + d].at[pl.ds(i * ND, ND)]
                 copy = pltpu.make_async_copy(part, mv.at[rows], in_sem.at[len(loads)])
                 copy.start()
                 loads.append(copy)
     zero = jnp.zeros((ROWS, LANES), jnp.float32)
     accs = (a0, a1, a2, a3)
 
-    def tile(row):
-        return pl.ds(pl.multiple_of(row, ROWS), ROWS)
-
     def clear(g, _):
         for acc in accs:
-            acc[tile(g * ROWS), :] = zero
+            acc[g] = zero
         return 0
 
     lax.fori_loop(0, nbins, clear, 0, unroll=8)
@@ -476,24 +472,16 @@
     for copy in loads:
         copy.wait()
 
-    def spread(g, shares_of):
-        for i in range(GROUP):
-            spots = [tile(spot_ref[4 * g + 4 * i + k]) for k in range(4)]
-            old = [acc[at, :] for acc, at in zip(accs, spots)]
-            for acc, at, was, add in zip(accs, spots, old, shares_of[4 * i : 4 * i + 4]):
-                acc[at, :] = was + add
-
-    def per_freq(f, carry):
+    def per_freq(f, steep):
         fr2, fr4, hspeed = ftab_ref[0, f], ftab_ref[1, f], ftab_ref[2, f]
 
-        def per_group(t, carry):
-            total, before = carry
+        def per_group(t, total):
             j0 = t * GROUP
             g0 = f * ND + j0
-            own = [mv[tile((g0 + i) * ROWS), :] for i in range(GROUP)]
-            found = [[mv[tile(spot_ref[4 * g0 + 4 * i + k]), :] for k in range(4)] for i in range(GROUP)]
-            spread(jnp.maximum(g0 - GROUP, 0), before)
-            shares_of = []
+            spots = [[spot_ref[4 * g0 + 4 * i + k] for k in range(4)] for i in range(GROUP)]
+            own = [mv[g0 + i] for i in range(GROUP)]
+            found = [[mv[b] for b in spots[i]] for i in range(GROUP)]
+            adds = []
             for i in range(GROUP):
                 m, (p0, p1, m0, m1) = own[i], found[i]
                 wp, wm = wts_ref[2 * g0 + 2 * i], wts_ref[2 * g0 + 2 * i + 1]
@@ -502,18 +490,20 @@
                 mf = fr4 * m
                 half = mf * (m * (ep * (1 / 1.25**4) + em * (1 / 0.75**4)) - ep * em * (2.0 / 0.9375**4))
                 drive = jnp.maximum(0.0, dw[j0 + i] - hspeed)
-                base[tile((g0 + i) * ROWS), :] = m + 0.15 * (drive * drive) * m - 2.0 * half
+                base[g0 + i] = m + 0.15 * (drive * drive) * m - 2.0 * half
                 sp, sm = wp * half, wm * half
-                shares_of += [sp, half - sp, sm, half - sm]
+                adds.append((sp, half - sp, sm, half - sm))
                 total = total + m
-            return total, tuple(shares_of)
-
-        steep, before = carry
-        part, before = lax.fori_loop(0, ND // GROUP, per_group, (zero, before), unroll=3)
-        return steep + part * fr2, before
-
-    steep, before = lax.fori_loop(0, nfreq, per_freq, (zero, (zero,) * (4 * GROUP)))
-    spread(nbins - GROUP, before)
+            for i in range(0, GROUP, 2):
+                for acc, b0, b1, x0, x1 in zip(accs, spots[i], spots[i + 1], adds[i], adds[i + 1]):
+                    old0, old1 = acc[b0], acc[b1]
+                    acc[b0] = old0 + x0
+                    acc[b1] = old1 + (x1 + jnp.where(b0 == b1, x0, zero))
+            return total
+
+        return steep + lax.fori_loop(0, ND // GROUP, per_group, zero, unroll=3) * fr2
+
+    steep = lax.fori_loop(0, nfreq, per_freq, zero)
     steep = steep * (1.0 / nbins)
     mask = mask_ref[...].astype(jnp.float32)
     per = nbins // PIECES
@@ -524,15 +514,15 @@
             g0 = t * ROWS
             done = []
             for i in range(ROWS):
-                at = tile((g0 + i) * ROWS)
-                mine = base[at, :] - (frs_ref[g0 + i] * steep) * mv[at, :]
-                done.append((mine + ((a0[at, :] + a1[at, :]) + (a2[at, :] + a3[at, :]))) * mask)
+                g = g0 + i
+                mine = base[g] - (frs_ref[g] * steep) * mv[g]
+                done.append((mine + ((a0[g] + a1[g]) + (a2[g] + a3[g]))) * mask)
             turned = jnp.swapaxes(jnp.stack(done, axis=0), 0, 1)
             for c in range(ROWS):
                 out_v[pl.ds(pl.multiple_of(g0, ROWS), ROWS), c * LANES : (c + 1) * LANES] = turned[c]
             return 0
 
-        lax.fori_loop(p * per // ROWS, (p + 1) * per // ROWS, finish, 0)
+        lax.fori_loop(p * per // ROWS, (p + 1) * per // ROWS, finish, 0, unroll=3)
         rows = pl.ds(p * per, per)
         copy = pltpu.make_async_copy(out_v.at[rows], out_hbm.at[rows], out_sem.at[p])
         copy.start()
@@ -548,9 +538,9 @@
     smem = pl.BlockSpec(memory_space=pltpu.SMEM)
     vmem = pl.BlockSpec(memory_space=pltpu.VMEM)
     points = ROWS * LANES
-    spots = (dia_bins * ROWS).T.reshape(-1)
+    spots = dia_bins.T.reshape(-1)
     wts = dia_wts.T.reshape(-1)
-    field = pltpu.VMEM((nbins * ROWS, LANES), jnp.float32)
+    field = pltpu.VMEM((nbins, ROWS, LANES), jnp.float32)
     return pl.pallas_call(
         functools.partial(tail_kernel, nfreq, bins_dev, plan),
         out_shape=jax.ShapeDtypeStruct((nbins, points), jnp.float32),
@@ -631,9 +621,10 @@
         blocks = front(speed_own, dirs, order, nbr, par, *halos[gi], slot, wet, ends, chunk, shares, kmin, kmax)
         arrived = []
         for d, block in enumerate(blocks):
-            rows = block.reshape(-1, LANES)
+            rows = block
             if d and parts:
-                rows, *_ = lax.optimization_barrier((rows,) + tuple(parts[-shares:][1:]))
+                before = parts[-shares:][1:] if c < len(plan) - 1 else [parts[d - shares]]
+                rows, *_ = lax.optimization_barrier((rows, *before))
             pairs = [(i, (i + d) % shares) for i in range(shares)]
             arrived.append(lax.ppermute(rows, "bin", pairs) if d else rows)
         earlier = tuple(parts[-shares:][1:]) if parts else (low_in, high_in) + sum(halos, ())

time: 200 us -> 193 us (0.965)
  Pallas kernels: 105 us -> 89.4 us
  waiting for transfers between devices: 48.4 us -> 58.8 us
  starting transfers between devices: 36 us -> 34 us
    pallas_call x4, Pallas kernels: 71.9 us -> 56.3 us  [front(): pl.pallas_call(functools.partial(front_kernel, tiles, shares, kmin, kmax,...]
    ppermute x12, waiting for transfers between devices: 45.5 us -> 55.4 us  [fast_on_device(): arrived.append(lax.ppermute(rows, 'bin', pairs) if d else rows)]
  transfers between devices with their start and end apart: 18 -> 18, of which waited for: 5 -> 6; matrix products, arithmetic and copies ran while one was open for 3% -> 3% of each run, Pallas kernels for 40% -> 33%
where the time goes in v1:
time: 193 us; the launch traced here: 190 us
  Pallas kernels  89.4 us (46%)
  waiting for transfers between devices  58.8 us (30%)
  starting transfers between devices  34 us (18%)
  local copies, waits for them, and re-layouts  7.22 us (4%)
    pallas_call x4, Pallas kernels, front(): pl.pallas_call(functools.partial(front_kernel, tiles, shares, kmin, kmax,...  56.3 us
    ppermute x12, waiting for transfers between devices, fast_on_device(): arrived.append(lax.ppermute(rows, 'bin', pairs) if d else rows)  55.4 us
    pallas_call x1, Pallas kernels, tail(): pl.pallas_call(functools.partial(tail_kernel, nfreq, bins_dev, plan), out...  23.2 us
    ppermute x12, starting transfers between devices, fast_on_device(): arrived.append(lax.ppermute(rows, 'bin', pairs) if d else rows)  17.6 us
    ppermute x6, starting transfers between devices, line(): return lax.ppermute(array, axis, pairs)  16.4 us
    pallas_call x2, Pallas kernels, prep(): pl.pallas_call(functools.partial(prep_kernel, points, bins, blocks, group...  9.88 us
  transfers between devices with their start and end apart: 18, of which 6 were waited for; matrix products, arithmetic and copies ran while one was open for 3% of the time, Pallas kernels for 33%

profile of v1, /device:TPU:1, one launch (start us, length us, event | category | flops | bytes accessed | tf_op | source)
XLA Modules:
  0.0 190.4 jit_solution(15004016832843890773)
XLA Ops:
  0.0 0.0 copy-start
  0.0 3.1 %prep.2 = (f32[2,592,128]{2,1,0:T(8,128)}, f32[2,592,128]{2,1,0:T(8,128)}) custom-call(f32[324,4096]{1,0:T(8,128)} %spec_hbm.2, s32[1,4096]{1,0:T(1,128)} %bitcast.38), custom_call_target="tpu_custom_call" | custom-call | bytes 6000000 | tf_op jit(solution)/shard_map/prep/pallas_call | solution.py:299
  3.1 4.5 %collective-permute-start = (f32[2,592,128]{2,1,0:T(8,128)}, f32[2,592,128]{2,1,0:T(8,128)S(1)}, u32[]{:S(2)}, u32[]{:S(2)}) collective-permute-start(f32[2,592,128]{2,1,0:T(8,128)} %get-tuple-element.43), channel_id=1, source_target_pairs={{0,4},{4,8},{8,12},{1,5},{5,9},{9,13},{2,6},{6,10},{10,14},{3,7},{... | collective-permute-start | bytes 1818632 | tf_op jit(solution)/shard_map/ppermute | solution.py:601
  7.7 0.0 copy-start.16
  7.7 0.0 copy-start.23
  7.7 0.0 copy-start.18
  7.7 0.0 copy-start.19
  7.7 0.0 copy-start.20
  7.7 0.0 copy-start.21
  7.8 2.1 %collective-permute-start.1 = (f32[2,592,128]{2,1,0:T(8,128)}, f32[2,592,128]{2,1,0:T(8,128)S(1)}, u32[]{:S(2)}, u32[]{:S(2)}) collective-permute-start(f32[2,592,128]{2,1,0:T(8,128)} %get-tuple-element.44), channel_id=1, source_target_pairs={{4,0},{8,4},{12,8},{5,1},{9,5},{13,9},{6,2},{10,6},{14,10},{7,3},{... | collective-permute-start | bytes 1818632 | tf_op jit(solution)/shard_map/ppermute | solution.py:601
  9.8 6.8 %prep.3 = (f32[7,592,128]{2,1,0:T(8,128)}, f32[7,592,128]{2,1,0:T(8,128)}, f32[10368,128]{1,0:T(8,128)}, f32[1152,128]{1,0:T(8,128)}, f32[1152,128]{1,0:T(8,128)}) custom-call(f32[324,4096]{1,0:T(8,128)} %spec_hbm.2, s32[1,4096]{1,0:T(1,128)} %bitcast.39), custom_call_target="tpu_custom_call" | custom-call | bytes 27000000 | tf_op jit(solution)/shard_map/prep/pallas_call | solution.py:299
  16.6 0.0 collective-permute-done.hs_ref
  16.6 2.9 %collective-permute-done.1.hn_ref = f32[2,592,128]{2,1,0:T(8,128)S(1)} collective-permute-done((f32[2,592,128]{2,1,0:T(8,128)}, f32[2,592,128]{2,1,0:T(8,128)S(1)}, u32[]{:S(2)}, u32[]{:S(2)}) %collective-permute-start.1) | collective-permute-done | bytes 606240 | tf_op jit(solution)/shard_map/ppermute | solution.py:601
  19.5 1.9 %collective-permute-start.7 = (f32[7,592,128]{2,1,0:T(8,128)}, f32[7,592,128]{2,1,0:T(8,128)S(1)}, u32[]{:S(2)}, u32[]{:S(2)}) collective-permute-start(f32[7,592,128]{2,1,0:T(8,128)} %get-tuple-element.55), channel_id=1, source_target_pairs={{0,4},{4,8},{8,12},{1,5},{5,9},{9,13},{2,6},{6,10},{10,14},{3,7},{... | collective-permute-start | bytes 6365192 | tf_op jit(solution)/shard_map/ppermute | solution.py:601
  21.4 2.5 %collective-permute-start.8 = (f32[7,592,128]{2,1,0:T(8,128)}, f32[7,592,128]{2,1,0:T(8,128)}, u32[]{:S(2)}, u32[]{:S(2)}) collective-permute-start(f32[7,592,128]{2,1,0:T(8,128)} %get-tuple-element.56), channel_id=1, source_target_pairs={{4,0},{8,4},{12,8},{5,1},{9,5},{13,9},{6,2},{10,6},{14,10},{7,3},{... | collective-permute-start | bytes 6365192 | tf_op jit(solution)/shard_map/ppermute | solution.py:601
  23.9 4.1 %collective-permute-start.5 = (f32[1152,128]{1,0:T(8,128)}, f32[1152,128]{1,0:T(8,128)}, u32[]{:S(2)}, u32[]{:S(2)}) collective-permute-start(f32[1152,128]{1,0:T(8,128)} %get-tuple-element.51), channel_id=1, source_target_pairs={{0,1},{1,2},{2,3},{4,5},{5,6},{6,7},{8,9},{9,10},{10,11},{12,13},{... | collective-permute-start | bytes 1769480 | tf_op jit(solution)/shard_map/ppermute | solution.py:601
  28.0 1.3 collective-permute-start.6
  29.3 0.0 copy-done.16
  29.3 0.6 copy.21
  30.0 0.6 dynamic_slice.11.tab_ref
  30.6 0.0 copy-done.18
  30.6 0.6 pad_maximum_fusion.par_ref
  31.2 12.8 %front.4 = (f32[72,8,128]{2,1,0:T(8,128)}, f32[72,8,128]{2,1,0:T(8,128)}, f32[72,8,128]{2,1,0:T(8,128)}, f32[72,8,128]{2,1,0:T(8,128)}) custom-call(f32[9]{0:T(128)} %dynamic_slice.11.tab_ref, f32[2,36]{1,0:T(2,128)} %constant.28.clone.dir_ref, s32[1]{0:T(128)} %bitcast.2.pos_ref, s32[4,32,128]{2,1,0:T(8,128)} %bitcast.34, ...), custom_call_target="tpu_custom_call" | custom-call | bytes 44000000 | tf_op jit(solution)/shard_map/front/pallas_call | solution.py:430
  44.1 2.1 %collective-permute-start.2 = (f32[72,8,128]{2,1,0:T(8,128)}, f32[72,8,128]{2,1,0:T(8,128)S(1)}, u32[]{:S(2)}, u32[]{:S(2)}) collective-permute-start(f32[72,8,128]{2,1,0:T(8,128)} %get-tuple-element.48), channel_id=1, source_target_pairs={{0,1},{1,2},{2,3},{3,0},{4,5},{5,6},{6,7},{7,4},{8,9},{9,10},{10,1... | collective-permute-start | bytes 884744 | tf_op jit(solution)/shard_map/ppermute | solution.py:629
  46.2 0.0 collective-permute-done.5
  46.2 2.3 %collective-permute-start.3 = (f32[72,8,128]{2,1,0:T(8,128)}, f32[72,8,128]{2,1,0:T(8,128)S(1)}, u32[]{:S(2)}, u32[]{:S(2)}) collective-permute-start(f32[72,8,128]{2,1,0:T(8,128)} %get-tuple-element.49), channel_id=1, source_target_pairs={{0,2},{1,3},{2,0},{3,1},{4,6},{5,7},{6,4},{7,5},{8,10},{9,11},{10,... | collective-permute-start | bytes 884744 | tf_op jit(solution)/shard_map/ppermute | solution.py:629
  48.5 0.0 collective-permute-done.6
  48.5 0.2 collective-permute-start.4
  48.7 0.0 collective-permute-done.7.hs_ref
  48.7 0.6 collective-permute-done.8.hn_ref
  49.3 0.7 copy-done.1
  50.1 12.9 %front.5 = (f32[72,8,128]{2,1,0:T(8,128)}, f32[72,8,128]{2,1,0:T(8,128)}, f32[72,8,128]{2,1,0:T(8,128)}, f32[72,8,128]{2,1,0:T(8,128)}) custom-call(f32[9]{0:T(128)} %dynamic_slice.11.tab_ref, f32[2,36]{1,0:T(2,128)} %constant.28.clone.dir_ref, s32[1]{0:T(128)} %bitcast.2.pos_ref, s32[4,32,128]{2,1,0:T(8,128)} %bitcast.35, ...), custom_call_target="tpu_custom_call" | custom-call | bytes 44000000 | tf_op jit(solution)/shard_map/front/pallas_call | solution.py:430
  62.9 0.0 collective-permute-done.2.refs_1_
  62.9 5.7 %collective-permute-done.3.refs_2_ = f32[72,8,128]{2,1,0:T(8,128)S(1)} collective-permute-done((f32[72,8,128]{2,1,0:T(8,128)}, f32[72,8,128]{2,1,0:T(8,128)S(1)}, u32[]{:S(2)}, u32[]{:S(2)}) %collective-permute-start.3) | collective-permute-done | bytes 294944 | tf_op jit(solution)/shard_map/ppermute | solution.py:629
  68.6 0.0 collective-permute-done.4.refs_3_
  68.6 6.6 %collective-permute-start.11 = (f32[72,8,128]{2,1,0:T(8,128)}, f32[72,8,128]{2,1,0:T(8,128)S(1)}, u32[]{:S(2)}, u32[]{:S(2)}) collective-permute-start(f32[72,8,128]{2,1,0:T(8,128)} %get-tuple-element.64), channel_id=1, source_target_pairs={{0,3},{1,0},{2,1},{3,2},{4,7},{5,4},{6,5},{7,6},{8,11},{9,8},{10,9... | collective-permute-start | bytes 884744 | tf_op jit(solution)/shard_map/ppermute | solution.py:629
  75.2 1.2 collective-permute-start.10
  76.4 0.0 collective-permute-start.9
  76.4 17.8 %front.6 = (f32[108,8,128]{2,1,0:T(8,128)}, f32[108,8,128]{2,1,0:T(8,128)}, f32[108,8,128]{2,1,0:T(8,128)}, f32[108,8,128]{2,1,0:T(8,128)}) custom-call(f32[9]{0:T(128)} %dynamic_slice.11.tab_ref, f32[2,36]{1,0:T(2,128)} %constant.28.clone.dir_ref, s32[1]{0:T(128)} %bitcast.2.pos_ref, s32[4,32,128]{2,1,0:T(8,128)} %bitcast.36, ...), custom_call_target="tpu_custom_call" | custom-call | bytes 66000000 | tf_op jit(solution)/shard_map/front/pallas_call | solution.py:430
  94.3 0.0 collective-permute-done.11.refs_7_
  94.3 7.9 %collective-permute-done.10.refs_6_ = f32[72,8,128]{2,1,0:T(8,128)S(1)} collective-permute-done((f32[72,8,128]{2,1,0:T(8,128)}, f32[72,8,128]{2,1,0:T(8,128)S(1)}, u32[]{:S(2)}, u32[]{:S(2)}) %collective-permute-start.10) | collective-permute-done | bytes 294944 | tf_op jit(solution)/shard_map/ppermute | solution.py:629
  102.2 0.0 collective-permute-done.9.refs_5_
  102.2 0.1 collective-permute-start.14
  102.3 0.7 collective-permute-start.13
  103.0 1.5 collective-permute-start.12
  104.5 12.8 %front.7 = (f32[72,8,128]{2,1,0:T(8,128)}, f32[72,8,128]{2,1,0:T(8,128)}, f32[72,8,128]{2,1,0:T(8,128)}, f32[72,8,128]{2,1,0:T(8,128)}) custom-call(f32[9]{0:T(128)} %dynamic_slice.11.tab_ref, f32[2,36]{1,0:T(2,128)} %constant.28.clone.dir_ref, s32[1]{0:T(128)} %bitcast.2.pos_ref, s32[4,32,128]{2,1,0:T(8,128)} %bitcast.37, ...), custom_call_target="tpu_custom_call" | custom-call | bytes 44000000 | tf_op jit(solution)/shard_map/front/pallas_call | solution.py:430
  117.4 0.0 collective-permute-done.14.refs_11_
  117.4 1.9 collective-permute-start.17
  119.3 28.1 %collective-permute-done.13.refs_10_ = f32[108,8,128]{2,1,0:T(8,128)S(1)} collective-permute-done((f32[108,8,128]{2,1,0:T(8,128)}, f32[108,8,128]{2,1,0:T(8,128)S(1)}, u32[]{:S(2)}, u32[]{:S(2)}) %collective-permute-start.13) | collective-permute-done | bytes 442400 | tf_op jit(solution)/shard_map/ppermute | solution.py:629
  147.4 0.0 collective-permute-start.16
  147.4 0.0 collective-permute-done.12.refs_9_
  147.4 1.1 collective-permute-start.15
  148.5 0.6 copy.22
  149.1 0.3 copy.15
  149.4 0.9 reshape.39.spot_ref
  150.3 0.3 copy.16
  150.6 0.9 reshape.40.wts_ref
  151.5 1.3 dynamic-slice_bitcast_fusion.1.mask_ref
  152.8 0.0 collective-permute-done.17.refs_15_
  152.8 13.6 %collective-permute-done.16.refs_14_ = f32[72,8,128]{2,1,0:T(8,128)S(1)} collective-permute-done((f32[72,8,128]{2,1,0:T(8,128)}, f32[72,8,128]{2,1,0:T(8,128)S(1)}, u32[]{:S(2)}, u32[]{:S(2)}) %collective-permute-start.16) | collective-permute-done | bytes 294944 | tf_op jit(solution)/shard_map/ppermute | solution.py:629
  166.4 0.0 collective-permute-done.15.refs_13_
  166.4 0.7 copy-done.14
  167.1 0.1 copy-done.15
  167.2 23.2 %tail.1 = f32[1296,1024]{1,0:T(8,128)} custom-call(s32[5184]{0:T(1024)} %reshape.39.spot_ref, f32[2592]{0:T(1024)} %reshape.40.wts_ref, f32[3,36]{1,0:T(4,128)} %constant.26.clone.ftab_ref, f32[1296]{0:T(1024)} %constant.27.clone.frs_ref, f32[2,36]{1,0:T(2,128)} %constant.28.clone.dir_ref, s32[1]{0:T(128)} %bitcast.2.pos_ref, f32[2,8,128]{2,1,0:T(8,128)} %bitcast.40, ...), custom_call_target="tpu_custom_call" | custom-call | bytes 70000000 | tf_op jit(solution)/shard_map/tail/pallas_call | solution.py:544
  (38 shorter events, 0.1 us)
Async XLA Ops:
  0.0 148.5 %copy-start = (f32[2,4096]{1,0:T(2,128)S(1)}, f32[2,4096]{1,0:T(2,128)}, u32[]{:S(2)}) copy-start(f32[2,4096]{1,0:T(2,128)} %param.15) | copy-start | bytes 98308
  3.1 13.4 %collective-permute-start = (f32[2,592,128]{2,1,0:T(8,128)}, f32[2,592,128]{2,1,0:T(8,128)S(1)}, u32[]{:S(2)}, u32[]{:S(2)}) collective-permute-start(f32[2,592,128]{2,1,0:T(8,128)} %get-tuple-element.43), channel_id=1, source_target_pairs={{0,4},{4,8},{8,12},{1,5},{5,9},{9,13},{2,6},{6,10},{10,14},{3,7},{... | collective-permute-start | bytes 1818632 | tf_op jit(solution)/shard_map/ppermute | solution.py:601
  7.7 21.6 %copy-start.16 = (s32[4,4096]{1,0:T(4,128)S(1)}, s32[4,4096]{1,0:T(4,128)}, u32[]{:S(2)}) copy-start(s32[4,4096]{1,0:T(4,128)} %param.17) | copy-start | bytes 196612
  7.7 22.3 %copy-start.23 = (f32[36]{0:T(128)S(1)}, f32[36]{0:T(128)}, u32[]{:S(2)}) copy-start(f32[36]{0:T(128)} %constant.25.clone) | copy-start | bytes 436
  7.7 22.9 %copy-start.18 = (f32[4096]{0:T(1024)S(1)}, f32[4096]{0:T(1024)}, u32[]{:S(2)}) copy-start(f32[4096]{0:T(1024)} %param.21) | copy-start | bytes 49156
  7.7 22.9 %copy-start.19 = (f32[4096]{0:T(1024)S(1)}, f32[4096]{0:T(1024)}, u32[]{:S(2)}) copy-start(f32[4096]{0:T(1024)} %param.20) | copy-start | bytes 49156
  7.7 22.9 %copy-start.20 = (f32[4096]{0:T(1024)S(1)}, f32[4096]{0:T(1024)}, u32[]{:S(2)}) copy-start(f32[4096]{0:T(1024)} %param.19) | copy-start | bytes 49156
  7.7 22.9 %copy-start.21 = (f32[4096]{0:T(1024)S(1)}, f32[4096]{0:T(1024)}, u32[]{:S(2)}) copy-start(f32[4096]{0:T(1024)} %param.18) | copy-start | bytes 49156
  7.8 11.7 %collective-permute-start.1 = (f32[2,592,128]{2,1,0:T(8,128)}, f32[2,592,128]{2,1,0:T(8,128)S(1)}, u32[]{:S(2)}, u32[]{:S(2)}) collective-permute-start(f32[2,592,128]{2,1,0:T(8,128)} %get-tuple-element.44), channel_id=1, source_target_pairs={{4,0},{8,4},{12,8},{5,1},{9,5},{13,9},{6,2},{10,6},{14,10},{7,3},{... | collective-permute-start | bytes 1818632 | tf_op jit(solution)/shard_map/ppermute | solution.py:601
  16.6 14.7 %copy-start.2 = (f32[2,592,128]{2,1,0:T(8,128)}, f32[2,592,128]{2,1,0:T(8,128)S(1)}, u32[]{:S(2)}) copy-start(f32[2,592,128]{2,1,0:T(8,128)S(1)} %collective-permute-done.hs_ref) | copy-start | bytes 1818628
  19.5 11.8 %copy-start.3 = (f32[2,592,128]{2,1,0:T(8,128)}, f32[2,592,128]{2,1,0:T(8,128)S(1)}, u32[]{:S(2)}) copy-start(f32[2,592,128]{2,1,0:T(8,128)S(1)} %collective-permute-done.1.hn_ref) | copy-start | bytes 1818628
  19.5 29.3 %collective-permute-start.7 = (f32[7,592,128]{2,1,0:T(8,128)}, f32[7,592,128]{2,1,0:T(8,128)S(1)}, u32[]{:S(2)}, u32[]{:S(2)}) collective-permute-start(f32[7,592,128]{2,1,0:T(8,128)} %get-tuple-element.55), channel_id=1, source_target_pairs={{0,4},{4,8},{8,12},{1,5},{5,9},{9,13},{2,6},{6,10},{10,14},{3,7},{... | collective-permute-start | bytes 6365192 | tf_op jit(solution)/shard_map/ppermute | solution.py:601
  21.4 27.9 %collective-permute-start.8 = (f32[7,592,128]{2,1,0:T(8,128)}, f32[7,592,128]{2,1,0:T(8,128)}, u32[]{:S(2)}, u32[]{:S(2)}) collective-permute-start(f32[7,592,128]{2,1,0:T(8,128)} %get-tuple-element.56), channel_id=1, source_target_pairs={{4,0},{8,4},{12,8},{5,1},{9,5},{13,9},{6,2},{10,6},{14,10},{7,3},{... | collective-permute-start | bytes 6365192 | tf_op jit(solution)/shard_map/ppermute | solution.py:601
  23.9 22.2 %collective-permute-start.5 = (f32[1152,128]{1,0:T(8,128)}, f32[1152,128]{1,0:T(8,128)}, u32[]{:S(2)}, u32[]{:S(2)}) collective-permute-start(f32[1152,128]{1,0:T(8,128)} %get-tuple-element.51), channel_id=1, source_target_pairs={{0,1},{1,2},{2,3},{4,5},{5,6},{6,7},{8,9},{9,10},{10,11},{12,13},{... | collective-permute-start | bytes 1769480 | tf_op jit(solution)/shard_map/ppermute | solution.py:601
  28.0 20.5 %collective-permute-start.6 = (f32[1152,128]{1,0:T(8,128)}, f32[1152,128]{1,0:T(8,128)}, u32[]{:S(2)}, u32[]{:S(2)}) collective-permute-start(f32[1152,128]{1,0:T(8,128)} %get-tuple-element.52), channel_id=1, source_target_pairs={{1,0},{2,1},{3,2},{5,4},{6,5},{7,6},{9,8},{10,9},{11,10},{13,12},{... | collective-permute-start | bytes 1769480 | tf_op jit(solution)/shard_map/ppermute | solution.py:601
  44.1 18.9 %collective-permute-start.2 = (f32[72,8,128]{2,1,0:T(8,128)}, f32[72,8,128]{2,1,0:T(8,128)S(1)}, u32[]{:S(2)}, u32[]{:S(2)}) collective-permute-start(f32[72,8,128]{2,1,0:T(8,128)} %get-tuple-element.48), channel_id=1, source_target_pairs={{0,1},{1,2},{2,3},{3,0},{4,5},{5,6},{6,7},{7,4},{8,9},{9,10},{10,1... | collective-permute-start | bytes 884744 | tf_op jit(solution)/shard_map/ppermute | solution.py:629
  46.2 22.4 %collective-permute-start.3 = (f32[72,8,128]{2,1,0:T(8,128)}, f32[72,8,128]{2,1,0:T(8,128)S(1)}, u32[]{:S(2)}, u32[]{:S(2)}) collective-permute-start(f32[72,8,128]{2,1,0:T(8,128)} %get-tuple-element.49), channel_id=1, source_target_pairs={{0,2},{1,3},{2,0},{3,1},{4,6},{5,7},{6,4},{7,5},{8,10},{9,11},{10,... | collective-permute-start | bytes 884744 | tf_op jit(solution)/shard_map/ppermute | solution.py:629
  48.5 20.1 %collective-permute-start.4 = (f32[72,8,128]{2,1,0:T(8,128)}, f32[72,8,128]{2,1,0:T(8,128)S(1)}, u32[]{:S(2)}, u32[]{:S(2)}) collective-permute-start(f32[72,8,128]{2,1,0:T(8,128)} %get-tuple-element.50), channel_id=1, source_target_pairs={{0,3},{1,0},{2,1},{3,2},{4,7},{5,4},{6,5},{7,6},{8,11},{9,8},{10,9... | collective-permute-start | bytes 884744 | tf_op jit(solution)/shard_map/ppermute | solution.py:629
  48.7 1.3 copy-start.1
  62.9 31.3 %copy-start.7 = (f32[72,8,128]{2,1,0:T(8,128)}, f32[72,8,128]{2,1,0:T(8,128)S(1)}, u32[]{:S(2)}) copy-start(f32[72,8,128]{2,1,0:T(8,128)S(1)} %collective-permute-done.2.refs_1_) | copy-start | bytes 884740
  68.6 25.6 %copy-start.8 = (f32[72,8,128]{2,1,0:T(8,128)}, f32[72,8,128]{2,1,0:T(8,128)S(1)}, u32[]{:S(2)}) copy-start(f32[72,8,128]{2,1,0:T(8,128)S(1)} %collective-permute-done.3.refs_2_) | copy-start | bytes 884740
  68.6 25.6 %copy-start.9 = (f32[72,8,128]{2,1,0:T(8,128)}, f32[72,8,128]{2,1,0:T(8,128)S(1)}, u32[]{:S(2)}) copy-start(f32[72,8,128]{2,1,0:T(8,128)S(1)} %collective-permute-done.4.refs_3_) | copy-start | bytes 884740
  68.6 25.6 %collective-permute-start.11 = (f32[72,8,128]{2,1,0:T(8,128)}, f32[72,8,128]{2,1,0:T(8,128)S(1)}, u32[]{:S(2)}, u32[]{:S(2)}) collective-permute-start(f32[72,8,128]{2,1,0:T(8,128)} %get-tuple-element.64), channel_id=1, source_target_pairs={{0,3},{1,0},{2,1},{3,2},{4,7},{5,4},{6,5},{7,6},{8,11},{9,8},{10,9... | collective-permute-start | bytes 884744 | tf_op jit(solution)/shard_map/ppermute | solution.py:629
  75.2 27.0 %collective-permute-start.10 = (f32[72,8,128]{2,1,0:T(8,128)}, f32[72,8,128]{2,1,0:T(8,128)S(1)}, u32[]{:S(2)}, u32[]{:S(2)}) collective-permute-start(f32[72,8,128]{2,1,0:T(8,128)} %get-tuple-element.62), channel_id=1, source_target_pairs={{0,2},{1,3},{2,0},{3,1},{4,6},{5,7},{6,4},{7,5},{8,10},{9,11},{10,... | collective-permute-start | bytes 884744 | tf_op jit(solution)/shard_map/ppermute | solution.py:629
  76.4 25.8 %collective-permute-start.9 = (f32[72,8,128]{2,1,0:T(8,128)}, f32[72,8,128]{2,1,0:T(8,128)S(1)}, u32[]{:S(2)}, u32[]{:S(2)}) collective-permute-start(f32[72,8,128]{2,1,0:T(8,128)} %get-tuple-element.60), channel_id=1, source_target_pairs={{0,1},{1,2},{2,3},{3,0},{4,5},{5,6},{6,7},{7,4},{8,9},{9,10},{10,1... | collective-permute-start | bytes 884744 | tf_op jit(solution)/shard_map/ppermute | solution.py:629
  94.3 23.1 %copy-start.10 = (f32[72,8,128]{2,1,0:T(8,128)}, f32[72,8,128]{2,1,0:T(8,128)S(1)}, u32[]{:S(2)}) copy-start(f32[72,8,128]{2,1,0:T(8,128)S(1)} %collective-permute-done.11.refs_7_) | copy-start | bytes 884740
  102.2 15.1 %copy-start.11 = (f32[72,8,128]{2,1,0:T(8,128)}, f32[72,8,128]{2,1,0:T(8,128)S(1)}, u32[]{:S(2)}) copy-start(f32[72,8,128]{2,1,0:T(8,128)S(1)} %collective-permute-done.10.refs_6_) | copy-start | bytes 884740
  102.2 15.1 %copy-start.12 = (f32[72,8,128]{2,1,0:T(8,128)}, f32[72,8,128]{2,1,0:T(8,128)S(1)}, u32[]{:S(2)}) copy-start(f32[72,8,128]{2,1,0:T(8,128)S(1)} %collective-permute-done.9.refs_5_) | copy-start | bytes 884740
  102.2 15.1 %collective-permute-start.14 = (f32[108,8,128]{2,1,0:T(8,128)}, f32[108,8,128]{2,1,0:T(8,128)S(1)}, u32[]{:S(2)}, u32[]{:S(2)}) collective-permute-start(f32[108,8,128]{2,1,0:T(8,128)} %get-tuple-element.72), channel_id=1, source_target_pairs={{0,3},{1,0},{2,1},{3,2},{4,7},{5,4},{6,5},{7,6},{8,11},{9,8},{10,9... | collective-permute-start | bytes 1327112 | tf_op jit(solution)/shard_map/ppermute | solution.py:629
  102.3 45.1 %collective-permute-start.13 = (f32[108,8,128]{2,1,0:T(8,128)}, f32[108,8,128]{2,1,0:T(8,128)S(1)}, u32[]{:S(2)}, u32[]{:S(2)}) collective-permute-start(f32[108,8,128]{2,1,0:T(8,128)} %get-tuple-element.70), channel_id=1, source_target_pairs={{0,2},{1,3},{2,0},{3,1},{4,6},{5,7},{6,4},{7,5},{8,10},{9,11},{10,... | collective-permute-start | bytes 1327112 | tf_op jit(solution)/shard_map/ppermute | solution.py:629
  103.0 44.4 %collective-permute-start.12 = (f32[108,8,128]{2,1,0:T(8,128)}, f32[108,8,128]{2,1,0:T(8,128)S(1)}, u32[]{:S(2)}, u32[]{:S(2)}) collective-permute-start(f32[108,8,128]{2,1,0:T(8,128)} %get-tuple-element.68), channel_id=1, source_target_pairs={{0,1},{1,2},{2,3},{3,0},{4,5},{5,6},{6,7},{7,4},{8,9},{9,10},{10,1... | collective-permute-start | bytes 1327112 | tf_op jit(solution)/shard_map/ppermute | solution.py:629
  104.5 44.6 %copy-start.17 = (s32[4,1296]{1,0:T(4,128)S(1)}, s32[4,1296]{1,0:T(4,128)}, u32[]{:S(2)}) copy-start(s32[4,1296]{1,0:T(4,128)} %param.22) | copy-start | bytes 62212
  104.5 45.8 %copy-start.22 = (f32[2,1296]{1,0:T(2,128)S(1)}, f32[2,1296]{1,0:T(2,128)}, u32[]{:S(2)}) copy-start(f32[2,1296]{1,0:T(2,128)} %param.23) | copy-start | bytes 31108
  117.4 49.0 %copy-start.4 = (f32[108,8,128]{2,1,0:T(8,128)}, f32[108,8,128]{2,1,0:T(8,128)S(1)}, u32[]{:S(2)}) copy-start(f32[108,8,128]{2,1,0:T(8,128)S(1)} %collective-permute-done.14.refs_11_) | copy-start | bytes 1327108
  117.4 35.4 %collective-permute-start.17 = (f32[72,8,128]{2,1,0:T(8,128)}, f32[72,8,128]{2,1,0:T(8,128)S(1)}, u32[]{:S(2)}, u32[]{:S(2)}) collective-permute-start(f32[72,8,128]{2,1,0:T(8,128)} %get-tuple-element.80), channel_id=1, source_target_pairs={{0,3},{1,0},{2,1},{3,2},{4,7},{5,4},{6,5},{7,6},{8,11},{9,8},{10,9... | collective-permute-start | bytes 884744 | tf_op jit(solution)/shard_map/ppermute | solution.py:629
  147.4 19.0 %copy-start.5 = (f32[108,8,128]{2,1,0:T(8,128)}, f32[108,8,128]{2,1,0:T(8,128)S(1)}, u32[]{:S(2)}) copy-start(f32[108,8,128]{2,1,0:T(8,128)S(1)} %collective-permute-done.13.refs_10_) | copy-start | bytes 1327108
  147.4 19.0 %collective-permute-start.16 = (f32[72,8,128]{2,1,0:T(8,128)}, f32[72,8,128]{2,1,0:T(8,128)S(1)}, u32[]{:S(2)}, u32[]{:S(2)}) collective-permute-start(f32[72,8,128]{2,1,0:T(8,128)} %get-tuple-element.78), channel_id=1, source_target_pairs={{0,2},{1,3},{2,0},{3,1},{4,6},{5,7},{6,4},{7,5},{8,10},{9,11},{10,... | collective-permute-start | bytes 884744 | tf_op jit(solution)/shard_map/ppermute | solution.py:629
  147.4 19.0 %copy-start.6 = (f32[108,8,128]{2,1,0:T(8,128)}, f32[108,8,128]{2,1,0:T(8,128)S(1)}, u32[]{:S(2)}) copy-start(f32[108,8,128]{2,1,0:T(8,128)S(1)} %collective-permute-done.12.refs_9_) | copy-start | bytes 1327108
  147.4 18.9 %collective-permute-start.15 = (f32[72,8,128]{2,1,0:T(8,128)}, f32[72,8,128]{2,1,0:T(8,128)S(1)}, u32[]{:S(2)}, u32[]{:S(2)}) collective-permute-start(f32[72,8,128]{2,1,0:T(8,128)} %get-tuple-element.76), channel_id=1, source_target_pairs={{0,1},{1,2},{2,3},{3,0},{4,5},{5,6},{6,7},{7,4},{8,9},{9,10},{10,1... | collective-permute-start | bytes 884744 | tf_op jit(solution)/shard_map/ppermute | solution.py:629
  152.8 13.6 %copy-start.13 = (f32[72,8,128]{2,1,0:T(8,128)}, f32[72,8,128]{2,1,0:T(8,128)S(1)}, u32[]{:S(2)}) copy-start(f32[72,8,128]{2,1,0:T(8,128)S(1)} %collective-permute-done.17.refs_15_) | copy-start | bytes 884740
  166.4 0.7 copy-start.14
  166.4 0.9 copy-start.15

commit v2 on v1

--- a/solution.py
+++ b/solution.py
@@ -168,6 +168,7 @@
 ROWS = 8
 EDGE = 16
 QUART = ND // 4
+APART = 3
 PIECES = 6
 VMEM_ASK = 60 << 20
 GROUP = 4
@@ -189,7 +190,7 @@
 
 
 def halo_groups(plan):
-    return [g for g in (plan[:1], plan[1:]) if g]
+    return [g for g in (plan[:1], plan[1:2], plan[2:]) if g]
 
 
 def slots_of(group):
@@ -317,19 +318,22 @@
 
 
 def front_kernel(
-    tiles, shares, kmin, kmax, chunk, edge, tab_ref, dir_ref, pos_ref, nbr_ref, par_ref, hs_ref, hn_ref, wet_ref, *refs
+    tiles, shares, nloc, kmin, kmax, chunk, edge, joined, tab_ref, dir_ref, pos_ref, nbr_ref, mx_ref, my_ref, rf_ref, fs_ref, hs_ref, hn_ref, wet_ref, *refs
 ):
-    near, outs, ext_ref = refs[: -shares - 1], refs[-shares - 1 : -1], refs[-1]
+    nout = 1 if joined else shares
+    near, outs, ext_ref = refs[: -nout - 1], refs[-nout - 1 : -1], refs[-1]
+    if joined:
+        outs = [outs[0].at[d] for d in range(shares)]
     place = pl.program_id(0)
-    speed = tab_ref[chunk[0] + chunk[1] * place]
+    speed = tab_ref[pos_ref[0] * nloc + chunk[0] + chunk[1] * place]
     first = place == 0
     half = ND // 2
     span = half * tiles
     south, north = tiles, ROWS
-    pitch = 2 * (2 * tiles + ROWS)
+    pitch = APART * (2 * tiles + ROWS)
 
     def rows_at(j, row, count=ROWS):
-        return pl.ds(j * pitch + 2 * row, count, stride=2)
+        return pl.ds(j * pitch + APART * row, count, stride=APART)
 
     def extend(q, _):
         for t in range(0, tiles, ROWS):
@@ -343,16 +347,16 @@
 
     lax.fori_loop(0, half, extend, 0, unroll=2)
     for q in range(QUART):
-        ext_ref[pl.ds((QUART + q) * pitch + 2 * (south + tiles), 1), :] = hn_ref[0, span + q : span + q + 1, :]
-        ext_ref[pl.ds((3 * QUART + q) * pitch + 2 * (north - 1), 1), :] = hs_ref[0, span + q : span + q + 1, :]
+        ext_ref[pl.ds((QUART + q) * pitch + APART * (south + tiles), 1), :] = hn_ref[0, span + q : span + q + 1, :]
+        ext_ref[pl.ds((3 * QUART + q) * pitch + APART * (north - 1), 1), :] = hs_ref[0, span + q : span + q + 1, :]
 
     side = jnp.where(first, 1.0, -1.0)
     per_share = tiles // shares
     steps = [(d, k) for d in range(shares) for k in range(per_share // ROWS)]
     firsts = {}
     for d, k in steps:
-        share = lax.rem(pos_ref[0] + d, shares)
-        firsts[d, k] = pl.multiple_of(share * per_share + k * ROWS, ROWS)
+        row = (d if joined else lax.rem(pos_ref[0] + d, shares)) * per_share + k * ROWS
+        firsts[d, k] = row if joined else pl.multiple_of(row, ROWS)
     sub = lax.broadcasted_iota(jnp.int32, (ROWS, LANES), 0)
     lanes, rels = {}, {}
     for way in range(4):
@@ -390,7 +394,7 @@
                 wet = wet_ref[0, j, at, :]
                 e_y = picked(j, own, step, way_y, off_y)
                 e_x = picked(j, own, step, way_x, off_x)
-                rf, fs = par_ref[2, at, :], par_ref[3, at, :]
+                rf, fs = rf_ref[at, :], fs_ref[at, :]
                 e_prev, e_next = wet_ref[0, jprev, at, :], wet_ref[0, jnext, at, :]
                 e_t = jnp.where(rf > 0, e_prev, e_next) if cos_up else jnp.where(rf < 0, e_prev, e_next)
                 if edge:
@@ -399,7 +403,7 @@
                     e_s = jnp.where(fs * side > 0, outer, inner)
                 else:
                     e_s = jnp.where(fs > 0, near[0][0, j, at, :], near[1][0, j, at, :])
-                spatial = (par_ref[0, at, :] * ax) * (wet - e_x) + (par_ref[1, at, :] * ay) * (wet - e_y)
+                spatial = (mx_ref[at, :] * ax) * (wet - e_x) + (my_ref[at, :] * ay) * (wet - e_y)
                 spectral = (jnp.abs(rf) * acos) * (wet - e_t) + (jnp.abs(fs) * speed) * (wet - e_s)
                 d, k = step
                 outs[d][j, k * ROWS : (k + 1) * ROWS, :] = wet - spatial - spectral
@@ -408,7 +412,7 @@
         lax.fori_loop(0, QUART, body, 0, unroll=3)
 
 
-def front(speed, dirs, pos, nbr, par, hs, hn, slot, wet, ends, chunk, shares, kmin, kmax):
+def front(speed, dirs, pos, nbr, par, hs, hn, slot, wet, ends, chunk, joined, shares, kmin, kmax):
     first, step, count = chunk
     tiles = nbr.shape[1]
     nloc = wet.shape[0]
@@ -427,35 +431,42 @@
     else:
         near, near_specs = (wet, wet), [freq_spec(first - 1, step), freq_spec(first + 1, step)]
     rows = tiles // shares
+    if joined:
+        outs = [jax.ShapeDtypeStruct((shares, count * ND, rows, LANES), jnp.float32)]
+        out_specs = [pl.BlockSpec((shares, ND, rows, LANES), lambda i: (0, i, 0, 0))]
+    else:
+        outs = [jax.ShapeDtypeStruct((count * ND, rows, LANES), jnp.float32)] * shares
+        out_specs = [pl.BlockSpec((ND, rows, LANES), lambda i: (i, 0, 0))] * shares
     return pl.pallas_call(
-        functools.partial(front_kernel, tiles, shares, kmin, kmax, chunk, bool(ends)),
+        functools.partial(front_kernel, tiles, shares, nloc, kmin, kmax, chunk, bool(ends), joined),
         grid=(count,),
-        out_shape=[jax.ShapeDtypeStruct((count * ND, rows, LANES), jnp.float32)] * shares,
+        out_shape=outs,
         in_specs=[smem] * 3
-        + [whole(nbr.shape), whole(par.shape), halo_spec, halo_spec, freq_spec(first, step)]
+        + [whole(nbr.shape)] + [whole(p.shape) for p in par] + [halo_spec, halo_spec, freq_spec(first, step)]
         + near_specs,
-        out_specs=[pl.BlockSpec((ND, rows, LANES), lambda i: (i, 0, 0))] * shares,
-        scratch_shapes=[pltpu.VMEM((ND * 2 * (2 * tiles + ROWS), LANES), jnp.float32)],
+        out_specs=out_specs,
+        scratch_shapes=[pltpu.VMEM((ND * APART * (2 * tiles + ROWS), LANES), jnp.float32)],
         compiler_params=pltpu.CompilerParams(vmem_limit_bytes=VMEM_ASK),
         cost_estimate=pl.CostEstimate(flops=0, bytes_accessed=count * 22_000_000, transcendentals=0),
         name="front",
-    )(speed, dirs, pos, nbr, par, hs, hn, wet, *near)
+    )(speed, dirs, pos, nbr, *par, hs, hn, wet, *near)
 
 
 def tail_kernel(nfreq, bins_dev, plan, spot_ref, wts_ref, ftab_ref, frs_ref, dir_ref, pos_ref, wind_ref, mask_ref, *refs):
     out_hbm, mv, base, a0, a1, a2, a3, dw, out_v, in_sem, out_sem = refs[-11:]
-    parts = refs[:-11]
-    nparts = len(parts)
-    shares = nparts // len(plan)
+    parts = iter(refs[:-11])
+    shares = nfreq * ND // bins_dev
     nbins = nfreq * ND
     loads = []
     for c, chunk in enumerate(plan):
+        joined = c == 0
+        whole = next(parts) if joined else None
         for d in range(shares):
-            source = lax.rem(pos_ref[0] + (shares - d), shares)
+            part = whole.at[d] if joined else next(parts)
+            source = d if joined else lax.rem(pos_ref[0] + (shares - d), shares)
             for i, f in enumerate(freqs_of(chunk)):
                 rows = pl.ds(source * bins_dev + f * ND, ND)
-                part = parts[c * shares + d].at[pl.ds(i * ND, ND)]
-                copy = pltpu.make_async_copy(part, mv.at[rows], in_sem.at[len(loads)])
+                copy = pltpu.make_async_copy(part.at[pl.ds(i * ND, ND)], mv.at[rows], in_sem.at[len(loads)])
                 copy.start()
                 loads.append(copy)
     zero = jnp.zeros((ROWS, LANES), jnp.float32)
@@ -582,7 +593,6 @@
     frs = jnp.asarray(np.repeat(3.0 * ratio, ND).astype(np.float32))
     theta = 2.0 * np.pi * (np.arange(ND) + 0.5) / ND
     dirs = jnp.asarray(np.stack([np.cos(theta), np.sin(theta)]).astype(np.float32))
-    speed_own = lax.dynamic_slice_in_dim(speed, bin_pos * nloc, nloc, 0)
 
     groups = halo_groups(plan)
     early = runs_of(slots_of(groups[0]))
@@ -600,36 +610,49 @@
             pairs = [(b, a) for a, b in pairs]
         return lax.ppermute(array, axis, pairs)
 
+    sends = list(zip(list(hs) + list(hs_rest), list(hn) + list(hn_rest)))
     halos = []
-    for south, north in zip(list(hs) + list(hs_rest), list(hn) + list(hn_rest)):
-        if halos:
-            south, north, *_ = lax.optimization_barrier((south, north) + halos[-1])
-        halos.append((line(south, "space", 1), line(north, "space", -1)))
+
+    def send_halos(*after):
+        if len(halos) < len(sends):
+            south, north = sends[len(halos)]
+            if after:
+                south, north, *_ = lax.optimization_barrier((south, north) + after)
+            halos.append((line(south, "space", 1), line(north, "space", -1)))
+
+    send_halos()
     low_in = line(low_out, "bin", 1).reshape(1, ND, tiles, LANES)
     high_in = line(high_out, "bin", -1).reshape(1, ND, tiles, LANES)
 
     nbr = (neighbours - space_pos * points).reshape(4, tiles, LANES)
-    par = jnp.stack([metric_x, metric_y, refraction, freq_shift]).reshape(4, tiles, LANES)
+    par = [p.reshape(tiles, LANES) for p in (metric_x, metric_y, refraction, freq_shift)]
     pos = bin_pos.reshape(1)
     kmin, kmax = points // 2, points
-    parts = []
+    arrived = []
     order = pos
     for c, chunk in enumerate(plan):
         first, step, count = chunk
+        joined = c == 0
         gi, slot = [(i, slots_of(g)[first]) for i, g in enumerate(groups) if chunk in g][0]
         ends = (low_in, high_in) if first == 0 else None
-        blocks = front(speed_own, dirs, order, nbr, par, *halos[gi], slot, wet, ends, chunk, shares, kmin, kmax)
-        arrived = []
-        for d, block in enumerate(blocks):
-            rows = block
-            if d and parts:
-                before = parts[-shares:][1:] if c < len(plan) - 1 else [parts[d - shares]]
+        blocks = front(speed, dirs, order, nbr, par, *halos[gi], slot, wet, ends, chunk, joined, shares, kmin, kmax)
+        if c == 0:
+            send_halos(low_in, high_in, blocks[0])
+            send_halos(*halos[-1])
+        earlier = arrived[-1] if arrived else [low_in, high_in]
+        order, *_ = lax.optimization_barrier((pos, blocks[0], *earlier))
+        if joined:
+            arrived.append([lax.all_to_all(blocks[0], "bin", split_axis=0, concat_axis=0, tiled=True)])
+            continue
+        here = [blocks[0]]
+        for d in range(1, shares):
+            rows = blocks[d]
+            if c > 1:
+                before = arrived[-1] if c < len(plan) - 1 else [arrived[-1][d]]
                 rows, *_ = lax.optimization_barrier((rows, *before))
-            pairs = [(i, (i + d) % shares) for i in range(shares)]
-            arrived.append(lax.ppermute(rows, "bin", pairs) if d else rows)
-        earlier = tuple(parts[-shares:][1:]) if parts else (low_in, high_in) + sum(halos, ())
-        order, *_ = lax.optimization_barrier((pos, blocks[0]) + earlier)
-        parts += arrived
+            here.append(lax.ppermute(rows, "bin", [(i, (i + d) % shares) for i in range(shares)]))
+        arrived.append(here)
+    parts = sum(arrived, [])
     wind_part = lax.dynamic_slice_in_dim(wind, bin_pos * share, share, 1).reshape(2, ROWS, LANES)
     mask_part = lax.dynamic_slice_in_dim(sea_mask, bin_pos * share, share, 0).reshape(ROWS, LANES)
     return tail(parts, plan, bins_dev, dia_bins, dia_wts, ftab, frs, dirs, pos, wind_part, mask_part)

time: 193 us -> 194 us (level)
  the two profiles are of different devices: /device:TPU:1 before, /device:TPU:21 now
where the time goes in v2:
time: 194 us; the launch traced here: 193 us
  Pallas kernels  89.1 us (46%)
  waiting for transfers between devices  54.3 us (28%)
  starting transfers between devices  39.4 us (20%)
  local copies, waits for them, and re-layouts  10 us (5%)
    pallas_call x4, Pallas kernels, front(): pl.pallas_call(functools.partial(front_kernel, tiles, shares, nloc, kmin,...  56.1 us
    ppermute x9, waiting for transfers between devices, fast_on_device(): lax.ppermute(rows, 'bin', [(i, (i + d) % shares) for i in range(shares)])  42.6 us
    ppermute x8, starting transfers between devices, line(): return lax.ppermute(array, axis, pairs)  23.7 us
    pallas_call x1, Pallas kernels, tail(): pl.pallas_call(functools.partial(tail_kernel, nfreq, bins_dev, plan), out...  23.2 us
    all_to_all x1, waiting for transfers between devices, fast_on_device(): lax.all_to_all(blocks[0], 'bin', split_axis=0, concat_axis=0, tiled=True)  11.6 us
    ppermute x9, starting transfers between devices, fast_on_device(): lax.ppermute(rows, 'bin', [(i, (i + d) % shares) for i in range(shares)])  11 us
    pallas_call x2, Pallas kernels, prep(): pl.pallas_call(functools.partial(prep_kernel, points, bins, blocks, group...  9.89 us
    unnamed x43, local copies, waits for them, and re-layouts  6.38 us
  transfers between devices with their start and end apart: 18, of which 4 were waited for; matrix products, arithmetic and copies ran while one was open for 3% of the time, Pallas kernels for 33%

profile of v2, /device:TPU:21, one launch (start us, length us, event | category | flops | bytes accessed | tf_op | source)
XLA Modules:
  0.0 193.2 jit_solution(15579205216837945024)
XLA Ops:
  0.0 0.0 copy-start
  0.0 3.1 %prep.2 = (f32[2,592,128]{2,1,0:T(8,128)}, f32[2,592,128]{2,1,0:T(8,128)}) custom-call(f32[324,4096]{1,0:T(8,128)} %spec_hbm.2, s32[1,4096]{1,0:T(1,128)} %bitcast.56), custom_call_target="tpu_custom_call" | custom-call | bytes 6000000 | tf_op jit(solution)/shard_map/prep/pallas_call | solution.py:300
  3.1 1.3 collective-permute-start
  4.4 0.0 copy-start.16
  4.5 3.4 %collective-permute-start.1 = (f32[2,592,128]{2,1,0:T(8,128)}, f32[2,592,128]{2,1,0:T(8,128)S(1)}, u32[]{:S(2)}, u32[]{:S(2)}) collective-permute-start(f32[2,592,128]{2,1,0:T(8,128)} %get-tuple-element.41), channel_id=1, source_target_pairs={{4,0},{8,4},{12,8},{5,1},{9,5},{13,9},{6,2},{10,6},{14,10},{7,3},{... | collective-permute-start | bytes 1818632 | tf_op jit(solution)/shard_map/ppermute | solution.py:611
  7.8 6.8 %prep.3 = (f32[2,592,128]{2,1,0:T(8,128)}, f32[5,592,128]{2,1,0:T(8,128)}, f32[2,592,128]{2,1,0:T(8,128)}, f32[5,592,128]{2,1,0:T(8,128)}, f32[10368,128]{1,0:T(...) custom-call(f32[324,4096]{1,0:T(8,128)} %spec_hbm.2, s32[1,4096]{1,0:T(1,128)} %bitcast.57), custom_call_target="tpu_custom_call" | custom-call | bytes 27000000 | tf_op jit(solution)/shard_map/prep/pallas_call | solution.py:300
  14.6 3.2 %collective-permute-start.2 = (f32[1152,128]{1,0:T(8,128)}, f32[1152,128]{1,0:T(8,128)S(1)}, u32[]{:S(2)}, u32[]{:S(2)}) collective-permute-start(f32[1152,128]{1,0:T(8,128)} %get-tuple-element.44), channel_id=1, source_target_pairs={{0,1},{1,2},{2,3},{4,5},{5,6},{6,7},{8,9},{9,10},{10,11},{12,13},{... | collective-permute-start | bytes 1769480 | tf_op jit(solution)/shard_map/ppermute | solution.py:611
  17.8 2.1 %collective-permute-start.3 = (f32[1152,128]{1,0:T(8,128)}, f32[1152,128]{1,0:T(8,128)S(1)}, u32[]{:S(2)}, u32[]{:S(2)}) collective-permute-start(f32[1152,128]{1,0:T(8,128)} %get-tuple-element.45), channel_id=1, source_target_pairs={{1,0},{2,1},{3,2},{5,4},{6,5},{7,6},{9,8},{10,9},{11,10},{13,12},{... | collective-permute-start | bytes 1769480 | tf_op jit(solution)/shard_map/ppermute | solution.py:611
  19.9 0.0 copy-done.16
  19.9 0.6 copy.21
  20.6 0.0 collective-permute-done.hs_ref
  20.6 0.0 collective-permute-done.1.hn_ref
  20.6 0.0 copy-start.4
  20.6 0.8 copy-done.3
  21.4 0.2 copy-done.4
  21.6 12.6 %front.4 = f32[4,72,8,128]{3,2,1,0:T(8,128)} custom-call(f32[36]{0:T(128)} %constant.21.clone.tab_ref, f32[2,36]{1,0:T(2,128)} %constant.24.clone.dir_ref, s32[1]{0:T(128)} %bitcast.2.pos_ref, s32[4,32,128]{2,1,0:T(8,128)} %bitcast.34, f32[32,128]{1,0:T(8,128)} %bitcast.40, f32[32,128]{1,0:T(8,128)} %bitcast.44, f32[32,128]{1,0:T(8,128)} %bitcast.48, ...), custom_call_target="tpu_custom_call" | custom-call | bytes 44000000 | tf_op jit(solution)/shard_map/front/pallas_call | solution.py:440
  34.2 0.0 collective-permute-done.2
  34.2 0.0 collective-permute-done.3
  34.2 1.3 collective-permute-start.4
  35.5 4.8 %collective-permute-start.5 = (f32[2,592,128]{2,1,0:T(8,128)S(1)}, f32[2,592,128]{2,1,0:T(8,128)S(1)}, u32[]{:S(2)}, u32[]{:S(2)}) collective-permute-start(f32[2,592,128]{2,1,0:T(8,128)S(1)} %copy-done.19), channel_id=1, source_target_pairs={{4,0},{8,4},{12,8},{5,1},{9,5},{13,9},{6,2},{10,6},{14,10},{7,3},{... | collective-permute-start | bytes 1818632 | tf_op jit(solution)/shard_map/ppermute | solution.py:611
  40.4 4.7 %all-to-all-start = ((f32[4,72,8,128]{3,2,1,0:T(8,128)}), f32[4,72,8,128]{3,2,1,0:T(8,128)}, u32[]{:S(2)}, u32[]{:S(2)}) async-start(f32[4,72,8,128]{3,2,1,0:T(8,128)} %front.4), calls=%async_computation | async-start | bytes 2359296 | tf_op jit(solution)/shard_map/all_to_all | solution.py:645
  45.1 0.0 collective-permute-done.4.hs_ref
  45.1 0.0 collective-permute-done.5.hn_ref
  45.1 0.8 copy-done.5
  45.9 0.2 copy-done.6
  46.2 0.0 copy-done.8
  46.2 6.3 %collective-permute-start.10 = (f32[5,592,128]{2,1,0:T(8,128)}, f32[5,592,128]{2,1,0:T(8,128)S(1)}, u32[]{:S(2)}, u32[]{:S(2)}) collective-permute-start(f32[5,592,128]{2,1,0:T(8,128)} %get-tuple-element.59), channel_id=1, source_target_pairs={{4,0},{8,4},{12,8},{5,1},{9,5},{13,9},{6,2},{10,6},{14,10},{7,3},{... | collective-permute-start | bytes 4546568 | tf_op jit(solution)/shard_map/ppermute | solution.py:611
  52.5 1.3 collective-permute-start.9
  53.8 12.8 %front.5 = (f32[72,8,128]{2,1,0:T(8,128)}, f32[72,8,128]{2,1,0:T(8,128)}, f32[72,8,128]{2,1,0:T(8,128)}, f32[72,8,128]{2,1,0:T(8,128)}) custom-call(f32[36]{0:T(128)} %constant.21.clone.tab_ref, f32[2,36]{1,0:T(2,128)} %constant.24.clone.dir_ref, s32[1]{0:T(128)} %bitcast.2.pos_ref, s32[4,32,128]{2,1,0:T(8,128)} %bitcast.35, f32[32,128]{1,0:T(8,128)} %bitcast.41, ...), custom_call_target="tpu_custom_call" | custom-call | bytes 44000000 | tf_op jit(solution)/shard_map/front/pallas_call | solution.py:440
  66.6 1.4 collective-permute-start.6
  67.9 0.1 collective-permute-start.7
  68.0 1.2 collective-permute-start.8
  69.2 11.6 %all-to-all-done.refs_0_ = f32[4,72,8,128]{3,2,1,0:T(8,128)} async-done(((f32[4,72,8,128]{3,2,1,0:T(8,128)}), f32[4,72,8,128]{3,2,1,0:T(8,128)}, u32[]{:S(2)}, u32[]{:S(2)}) %all-to-all-start) | async-done | bytes 1179680 | tf_op jit(solution)/shard_map/all_to_all | solution.py:645
  80.8 0.0 collective-permute-done.10.hn_ref
  80.8 0.0 collective-permute-done.9.hs_ref
  80.8 1.1 copy-done.1
  81.9 1.2 copy-done.2
  83.1 17.8 %front.6 = (f32[108,8,128]{2,1,0:T(8,128)}, f32[108,8,128]{2,1,0:T(8,128)}, f32[108,8,128]{2,1,0:T(8,128)}, f32[108,8,128]{2,1,0:T(8,128)}) custom-call(f32[36]{0:T(128)} %constant.21.clone.tab_ref, f32[2,36]{1,0:T(2,128)} %constant.24.clone.dir_ref, s32[1]{0:T(128)} %bitcast.2.pos_ref, s32[4,32,128]{2,1,0:T(8,128)} %bitcast.36, f32[32,128]{1,0:T(8,128)} %bitcast.42, ...), custom_call_target="tpu_custom_call" | custom-call | bytes 66000000 | tf_op jit(solution)/shard_map/front/pallas_call | solution.py:440
  100.9 0.0 collective-permute-done.6.refs_2_
  100.9 0.0 collective-permute-done.7.refs_3_
  100.9 0.0 collective-permute-done.8.refs_4_
  101.0 0.1 collective-permute-start.13
  101.0 3.7 %collective-permute-start.12 = (f32[108,8,128]{2,1,0:T(8,128)}, f32[108,8,128]{2,1,0:T(8,128)S(1)}, u32[]{:S(2)}, u32[]{:S(2)}) collective-permute-start(f32[108,8,128]{2,1,0:T(8,128)} %get-tuple-element.64), channel_id=1, source_target_pairs={{0,2},{1,3},{2,0},{3,1},{4,6},{5,7},{6,4},{7,5},{8,10},{9,11},{10,... | collective-permute-start | bytes 1327112 | tf_op jit(solution)/shard_map/ppermute | solution.py:653
  104.7 1.4 collective-permute-start.11
  106.1 12.9 %front.7 = (f32[72,8,128]{2,1,0:T(8,128)}, f32[72,8,128]{2,1,0:T(8,128)}, f32[72,8,128]{2,1,0:T(8,128)}, f32[72,8,128]{2,1,0:T(8,128)}) custom-call(f32[36]{0:T(128)} %constant.21.clone.tab_ref, f32[2,36]{1,0:T(2,128)} %constant.24.clone.dir_ref, s32[1]{0:T(128)} %bitcast.2.pos_ref, s32[4,32,128]{2,1,0:T(8,128)} %bitcast.37, f32[32,128]{1,0:T(8,128)} %bitcast.43, ...), custom_call_target="tpu_custom_call" | custom-call | bytes 44000000 | tf_op jit(solution)/shard_map/front/pallas_call | solution.py:440
  119.0 0.0 copy-done.12
  119.0 0.0 collective-permute-done.13.refs_8_
  119.0 0.1 collective-permute-start.16
  119.1 15.9 %collective-permute-done.12.refs_7_ = f32[108,8,128]{2,1,0:T(8,128)S(1)} collective-permute-done((f32[108,8,128]{2,1,0:T(8,128)}, f32[108,8,128]{2,1,0:T(8,128)S(1)}, u32[]{:S(2)}, u32[]{:S(2)}) %collective-permute-start.12) | collective-permute-done | bytes 442400 | tf_op jit(solution)/shard_map/ppermute | solution.py:653
  135.0 3.1 %collective-permute-start.15 = (f32[72,8,128]{2,1,0:T(8,128)}, f32[72,8,128]{2,1,0:T(8,128)S(1)}, u32[]{:S(2)}, u32[]{:S(2)}) collective-permute-start(f32[72,8,128]{2,1,0:T(8,128)} %get-tuple-element.72), channel_id=1, source_target_pairs={{0,2},{1,3},{2,0},{3,1},{4,6},{5,7},{6,4},{7,5},{8,10},{9,11},{10,... | collective-permute-start | bytes 884744 | tf_op jit(solution)/shard_map/ppermute | solution.py:653
  138.2 15.2 %collective-permute-done.11.refs_6_ = f32[108,8,128]{2,1,0:T(8,128)S(1)} collective-permute-done((f32[108,8,128]{2,1,0:T(8,128)}, f32[108,8,128]{2,1,0:T(8,128)S(1)}, u32[]{:S(2)}, u32[]{:S(2)}) %collective-permute-start.11) | collective-permute-done | bytes 442400 | tf_op jit(solution)/shard_map/ppermute | solution.py:653
  153.4 0.0 collective-permute-start.14
  153.4 0.7 copy.22
  154.1 0.3 copy.15
  154.4 0.9 reshape.42.spot_ref
  155.3 0.3 copy.16
  155.6 0.9 reshape.43.wts_ref
  156.5 1.3 dynamic-slice_bitcast_fusion.1.mask_ref
  157.8 0.0 collective-permute-done.16.refs_12_
  157.8 0.0 collective-permute-done.15.refs_11_
  157.8 0.0 copy-start.14
  157.8 11.4 %collective-permute-done.14.refs_10_ = f32[72,8,128]{2,1,0:T(8,128)S(1)} collective-permute-done((f32[72,8,128]{2,1,0:T(8,128)}, f32[72,8,128]{2,1,0:T(8,128)S(1)}, u32[]{:S(2)}, u32[]{:S(2)}) %collective-permute-start.14) | collective-permute-done | bytes 294944 | tf_op jit(solution)/shard_map/ppermute | solution.py:653
  169.3 0.7 copy-done.15
  170.0 23.2 %tail.1 = f32[1296,1024]{1,0:T(8,128)} custom-call(s32[5184]{0:T(1024)} %reshape.42.spot_ref, f32[2592]{0:T(1024)} %reshape.43.wts_ref, f32[3,36]{1,0:T(4,128)} %constant.22.clone.ftab_ref, f32[1296]{0:T(1024)} %constant.23.clone.frs_ref, f32[2,36]{1,0:T(2,128)} %constant.24.clone.dir_ref, s32[1]{0:T(128)} %bitcast.2.pos_ref, f32[2,8,128]{2,1,0:T(8,128)} %bitcast.58, ...), custom_call_target="tpu_custom_call" | custom-call | bytes 70000000 | tf_op jit(solution)/shard_map/tail/pallas_call | solution.py:555
  (28 shorter events, 0.1 us)
Async XLA Ops:
  0.0 153.4 %copy-start = (f32[2,4096]{1,0:T(2,128)S(1)}, f32[2,4096]{1,0:T(2,128)}, u32[]{:S(2)}) copy-start(f32[2,4096]{1,0:T(2,128)} %param.15) | copy-start | bytes 98308
  3.1 17.4 %collective-permute-start = (f32[2,592,128]{2,1,0:T(8,128)}, f32[2,592,128]{2,1,0:T(8,128)S(1)}, u32[]{:S(2)}, u32[]{:S(2)}) collective-permute-start(f32[2,592,128]{2,1,0:T(8,128)} %get-tuple-element.40), channel_id=1, source_target_pairs={{0,4},{4,8},{8,12},{1,5},{5,9},{9,13},{2,6},{6,10},{10,14},{3,7},{... | collective-permute-start | bytes 1818632 | tf_op jit(solution)/shard_map/ppermute | solution.py:611
  4.4 15.5 %copy-start.16 = (s32[4,4096]{1,0:T(4,128)S(1)}, s32[4,4096]{1,0:T(4,128)}, u32[]{:S(2)}) copy-start(s32[4,4096]{1,0:T(4,128)} %param.17) | copy-start | bytes 196612
  4.5 16.1 %collective-permute-start.1 = (f32[2,592,128]{2,1,0:T(8,128)}, f32[2,592,128]{2,1,0:T(8,128)S(1)}, u32[]{:S(2)}, u32[]{:S(2)}) collective-permute-start(f32[2,592,128]{2,1,0:T(8,128)} %get-tuple-element.41), channel_id=1, source_target_pairs={{4,0},{8,4},{12,8},{5,1},{9,5},{13,9},{6,2},{10,6},{14,10},{7,3},{... | collective-permute-start | bytes 1818632 | tf_op jit(solution)/shard_map/ppermute | solution.py:611
  14.6 19.6 %collective-permute-start.2 = (f32[1152,128]{1,0:T(8,128)}, f32[1152,128]{1,0:T(8,128)S(1)}, u32[]{:S(2)}, u32[]{:S(2)}) collective-permute-start(f32[1152,128]{1,0:T(8,128)} %get-tuple-element.44), channel_id=1, source_target_pairs={{0,1},{1,2},{2,3},{4,5},{5,6},{6,7},{8,9},{9,10},{10,11},{12,13},{... | collective-permute-start | bytes 1769480 | tf_op jit(solution)/shard_map/ppermute | solution.py:611
  17.8 16.4 %collective-permute-start.3 = (f32[1152,128]{1,0:T(8,128)}, f32[1152,128]{1,0:T(8,128)S(1)}, u32[]{:S(2)}, u32[]{:S(2)}) collective-permute-start(f32[1152,128]{1,0:T(8,128)} %get-tuple-element.45), channel_id=1, source_target_pairs={{1,0},{2,1},{3,2},{5,4},{6,5},{7,6},{9,8},{10,9},{11,10},{13,12},{... | collective-permute-start | bytes 1769480 | tf_op jit(solution)/shard_map/ppermute | solution.py:611
  20.6 0.8 copy-start.3
  20.6 1.0 copy-start.4
  21.6 14.0 %copy-start.19 = (f32[2,592,128]{2,1,0:T(8,128)S(1)}, f32[2,592,128]{2,1,0:T(8,128)}, u32[]{:S(2)}) copy-start(f32[2,592,128]{2,1,0:T(8,128)} %get-tuple-element.50) | copy-start | bytes 1818628
  34.2 10.9 %copy-start.7 = (f32[1152,128]{1,0:T(8,128)}, f32[1152,128]{1,0:T(8,128)S(1)}, u32[]{:S(2)}) copy-start(f32[1152,128]{1,0:T(8,128)S(1)} %collective-permute-done.2) | copy-start | bytes 1769476
  34.2 11.9 %copy-start.8 = (f32[1152,128]{1,0:T(8,128)}, f32[1152,128]{1,0:T(8,128)S(1)}, u32[]{:S(2)}) copy-start(f32[1152,128]{1,0:T(8,128)S(1)} %collective-permute-done.3) | copy-start | bytes 1769476
  34.2 10.8 %collective-permute-start.4 = (f32[2,592,128]{2,1,0:T(8,128)}, f32[2,592,128]{2,1,0:T(8,128)S(1)}, u32[]{:S(2)}, u32[]{:S(2)}) collective-permute-start(f32[2,592,128]{2,1,0:T(8,128)} %get-tuple-element.49), channel_id=1, source_target_pairs={{0,4},{4,8},{8,12},{1,5},{5,9},{9,13},{2,6},{6,10},{10,14},{3,7},{... | collective-permute-start | bytes 1818632 | tf_op jit(solution)/shard_map/ppermute | solution.py:611
  35.5 9.5 %collective-permute-start.5 = (f32[2,592,128]{2,1,0:T(8,128)S(1)}, f32[2,592,128]{2,1,0:T(8,128)S(1)}, u32[]{:S(2)}, u32[]{:S(2)}) collective-permute-start(f32[2,592,128]{2,1,0:T(8,128)S(1)} %copy-done.19), channel_id=1, source_target_pairs={{4,0},{8,4},{12,8},{5,1},{9,5},{13,9},{6,2},{10,6},{14,10},{7,3},{... | collective-permute-start | bytes 1818632 | tf_op jit(solution)/shard_map/ppermute | solution.py:611
  40.4 40.4 %all-to-all-start = ((f32[4,72,8,128]{3,2,1,0:T(8,128)}), f32[4,72,8,128]{3,2,1,0:T(8,128)}, u32[]{:S(2)}, u32[]{:S(2)}) async-start(f32[4,72,8,128]{3,2,1,0:T(8,128)} %front.4), calls=%async_computation | async-start | bytes 2359296 | tf_op jit(solution)/shard_map/all_to_all | solution.py:645
  45.1 0.8 copy-start.5
  45.1 1.1 copy-start.6
  46.2 34.7 %collective-permute-start.10 = (f32[5,592,128]{2,1,0:T(8,128)}, f32[5,592,128]{2,1,0:T(8,128)S(1)}, u32[]{:S(2)}, u32[]{:S(2)}) collective-permute-start(f32[5,592,128]{2,1,0:T(8,128)} %get-tuple-element.59), channel_id=1, source_target_pairs={{4,0},{8,4},{12,8},{5,1},{9,5},{13,9},{6,2},{10,6},{14,10},{7,3},{... | collective-permute-start | bytes 4546568 | tf_op jit(solution)/shard_map/ppermute | solution.py:611
  52.5 28.3 %collective-permute-start.9 = (f32[5,592,128]{2,1,0:T(8,128)}, f32[5,592,128]{2,1,0:T(8,128)S(1)}, u32[]{:S(2)}, u32[]{:S(2)}) collective-permute-start(f32[5,592,128]{2,1,0:T(8,128)} %get-tuple-element.58), channel_id=1, source_target_pairs={{0,4},{4,8},{8,12},{1,5},{5,9},{9,13},{2,6},{6,10},{10,14},{3,7},{... | collective-permute-start | bytes 4546568 | tf_op jit(solution)/shard_map/ppermute | solution.py:611
  66.6 34.3 %collective-permute-start.6 = (f32[72,8,128]{2,1,0:T(8,128)}, f32[72,8,128]{2,1,0:T(8,128)S(1)}, u32[]{:S(2)}, u32[]{:S(2)}) collective-permute-start(f32[72,8,128]{2,1,0:T(8,128)} %get-tuple-element.52), channel_id=1, source_target_pairs={{0,1},{1,2},{2,3},{3,0},{4,5},{5,6},{6,7},{7,4},{8,9},{9,10},{10,1... | collective-permute-start | bytes 884744 | tf_op jit(solution)/shard_map/ppermute | solution.py:653
  67.9 33.0 %collective-permute-start.7 = (f32[72,8,128]{2,1,0:T(8,128)}, f32[72,8,128]{2,1,0:T(8,128)}, u32[]{:S(2)}, u32[]{:S(2)}) collective-permute-start(f32[72,8,128]{2,1,0:T(8,128)} %get-tuple-element.53), channel_id=1, source_target_pairs={{0,2},{1,3},{2,0},{3,1},{4,6},{5,7},{6,4},{7,5},{8,10},{9,11},{10,... | collective-permute-start | bytes 884744 | tf_op jit(solution)/shard_map/ppermute | solution.py:653
  68.0 33.0 %collective-permute-start.8 = (f32[72,8,128]{2,1,0:T(8,128)}, f32[72,8,128]{2,1,0:T(8,128)}, u32[]{:S(2)}, u32[]{:S(2)}) collective-permute-start(f32[72,8,128]{2,1,0:T(8,128)} %get-tuple-element.54), channel_id=1, source_target_pairs={{0,3},{1,0},{2,1},{3,2},{4,7},{5,4},{6,5},{7,6},{8,11},{9,8},{10,9... | collective-permute-start | bytes 884744 | tf_op jit(solution)/shard_map/ppermute | solution.py:653
  80.8 1.1 copy-start.1
  81.9 1.2 copy-start.2
  100.9 18.0 %copy-start.12 = (f32[72,8,128]{2,1,0:T(8,128)}, f32[72,8,128]{2,1,0:T(8,128)S(1)}, u32[]{:S(2)}) copy-start(f32[72,8,128]{2,1,0:T(8,128)S(1)} %collective-permute-done.6.refs_2_) | copy-start | bytes 884740
  101.0 18.0 %collective-permute-start.13 = (f32[108,8,128]{2,1,0:T(8,128)}, f32[108,8,128]{2,1,0:T(8,128)S(1)}, u32[]{:S(2)}, u32[]{:S(2)}) collective-permute-start(f32[108,8,128]{2,1,0:T(8,128)} %get-tuple-element.66), channel_id=1, source_target_pairs={{0,3},{1,0},{2,1},{3,2},{4,7},{5,4},{6,5},{7,6},{8,11},{9,8},{10,9... | collective-permute-start | bytes 1327112 | tf_op jit(solution)/shard_map/ppermute | solution.py:653
  101.0 34.0 %collective-permute-start.12 = (f32[108,8,128]{2,1,0:T(8,128)}, f32[108,8,128]{2,1,0:T(8,128)S(1)}, u32[]{:S(2)}, u32[]{:S(2)}) collective-permute-start(f32[108,8,128]{2,1,0:T(8,128)} %get-tuple-element.64), channel_id=1, source_target_pairs={{0,2},{1,3},{2,0},{3,1},{4,6},{5,7},{6,4},{7,5},{8,10},{9,11},{10,... | collective-permute-start | bytes 1327112 | tf_op jit(solution)/shard_map/ppermute | solution.py:653
  104.7 48.7 %collective-permute-start.11 = (f32[108,8,128]{2,1,0:T(8,128)}, f32[108,8,128]{2,1,0:T(8,128)S(1)}, u32[]{:S(2)}, u32[]{:S(2)}) collective-permute-start(f32[108,8,128]{2,1,0:T(8,128)} %get-tuple-element.62), channel_id=1, source_target_pairs={{0,1},{1,2},{2,3},{3,0},{4,5},{5,6},{6,7},{7,4},{8,9},{9,10},{10,1... | collective-permute-start | bytes 1327112 | tf_op jit(solution)/shard_map/ppermute | solution.py:653
  106.1 48.0 %copy-start.17 = (s32[4,1296]{1,0:T(4,128)S(1)}, s32[4,1296]{1,0:T(4,128)}, u32[]{:S(2)}) copy-start(s32[4,1296]{1,0:T(4,128)} %param.22) | copy-start | bytes 62212
  106.1 49.2 %copy-start.18 = (f32[2,1296]{1,0:T(2,128)S(1)}, f32[2,1296]{1,0:T(2,128)}, u32[]{:S(2)}) copy-start(f32[2,1296]{1,0:T(2,128)} %param.23) | copy-start | bytes 31108
  119.0 50.3 %copy-start.9 = (f32[108,8,128]{2,1,0:T(8,128)}, f32[108,8,128]{2,1,0:T(8,128)S(1)}, u32[]{:S(2)}) copy-start(f32[108,8,128]{2,1,0:T(8,128)S(1)} %collective-permute-done.13.refs_8_) | copy-start | bytes 1327108
  119.0 38.8 %collective-permute-start.16 = (f32[72,8,128]{2,1,0:T(8,128)}, f32[72,8,128]{2,1,0:T(8,128)S(1)}, u32[]{:S(2)}, u32[]{:S(2)}) collective-permute-start(f32[72,8,128]{2,1,0:T(8,128)} %get-tuple-element.74), channel_id=1, source_target_pairs={{0,3},{1,0},{2,1},{3,2},{4,7},{5,4},{6,5},{7,6},{8,11},{9,8},{10,9... | collective-permute-start | bytes 884744 | tf_op jit(solution)/shard_map/ppermute | solution.py:653
  135.0 34.2 %copy-start.10 = (f32[108,8,128]{2,1,0:T(8,128)}, f32[108,8,128]{2,1,0:T(8,128)S(1)}, u32[]{:S(2)}) copy-start(f32[108,8,128]{2,1,0:T(8,128)S(1)} %collective-permute-done.12.refs_7_) | copy-start | bytes 1327108
  135.0 22.8 %collective-permute-start.15 = (f32[72,8,128]{2,1,0:T(8,128)}, f32[72,8,128]{2,1,0:T(8,128)S(1)}, u32[]{:S(2)}, u32[]{:S(2)}) collective-permute-start(f32[72,8,128]{2,1,0:T(8,128)} %get-tuple-element.72), channel_id=1, source_target_pairs={{0,2},{1,3},{2,0},{3,1},{4,6},{5,7},{6,4},{7,5},{8,10},{9,11},{10,... | collective-permute-start | bytes 884744 | tf_op jit(solution)/shard_map/ppermute | solution.py:653
  153.4 15.9 %copy-start.11 = (f32[108,8,128]{2,1,0:T(8,128)}, f32[108,8,128]{2,1,0:T(8,128)S(1)}, u32[]{:S(2)}) copy-start(f32[108,8,128]{2,1,0:T(8,128)S(1)} %collective-permute-done.11.refs_6_) | copy-start | bytes 1327108
  153.4 15.8 %collective-permute-start.14 = (f32[72,8,128]{2,1,0:T(8,128)}, f32[72,8,128]{2,1,0:T(8,128)S(1)}, u32[]{:S(2)}, u32[]{:S(2)}) collective-permute-start(f32[72,8,128]{2,1,0:T(8,128)} %get-tuple-element.70), channel_id=1, source_target_pairs={{0,1},{1,2},{2,3},{3,0},{4,5},{5,6},{6,7},{7,4},{8,9},{9,10},{10,1... | collective-permute-start | bytes 884744 | tf_op jit(solution)/shard_map/ppermute | solution.py:653
  157.8 11.5 %copy-start.13 = (f32[72,8,128]{2,1,0:T(8,128)}, f32[72,8,128]{2,1,0:T(8,128)S(1)}, u32[]{:S(2)}) copy-start(f32[72,8,128]{2,1,0:T(8,128)S(1)} %collective-permute-done.16.refs_12_) | copy-start | bytes 884740
  157.8 11.5 %copy-start.14 = (f32[72,8,128]{2,1,0:T(8,128)}, f32[72,8,128]{2,1,0:T(8,128)S(1)}, u32[]{:S(2)}) copy-start(f32[72,8,128]{2,1,0:T(8,128)S(1)} %collective-permute-done.15.refs_11_) | copy-start | bytes 884740
  169.3 0.7 copy-start.15

commit v3 on v2

--- a/solution.py
+++ b/solution.py
@@ -621,6 +621,7 @@
             halos.append((line(south, "space", 1), line(north, "space", -1)))
 
     send_halos()
+    send_halos()
     low_in = line(low_out, "bin", 1).reshape(1, ND, tiles, LANES)
     high_in = line(high_out, "bin", -1).reshape(1, ND, tiles, LANES)
 
@@ -638,7 +639,6 @@
         blocks = front(speed, dirs, order, nbr, par, *halos[gi], slot, wet, ends, chunk, joined, shares, kmin, kmax)
         if c == 0:
             send_halos(low_in, high_in, blocks[0])
-            send_halos(*halos[-1])
         earlier = arrived[-1] if arrived else [low_in, high_in]
         order, *_ = lax.optimization_barrier((pos, blocks[0], *earlier))
         if joined:

time: 194 us -> 191 us (0.985)
  the two profiles are of different devices: /device:TPU:21 before, /device:TPU:1 now
where the time goes in v3:
time: 191 us; the launch traced here: 190 us
  Pallas kernels  89.1 us (47%)
  waiting for transfers between devices  45.8 us (24%)
  starting transfers between devices  44.1 us (23%)
  local copies, waits for them, and re-layouts  10.3 us (5%)
    pallas_call x4, Pallas kernels, front(): pl.pallas_call(functools.partial(front_kernel, tiles, shares, nloc, kmin,...  56 us
    ppermute x9, waiting for transfers between devices, fast_on_device(): lax.ppermute(rows, 'bin', [(i, (i + d) % shares) for i in range(shares)])  27.4 us
    pallas_call x1, Pallas kernels, tail(): pl.pallas_call(functools.partial(tail_kernel, nfreq, bins_dev, plan), out...  23.2 us
    ppermute x8, starting transfers between devices, line(): return lax.ppermute(array, axis, pairs)  22.6 us
    ppermute x8, waiting for transfers between devices, line(): return lax.ppermute(array, axis, pairs)  18.4 us
    ppermute x9, starting transfers between devices, fast_on_device(): lax.ppermute(rows, 'bin', [(i, (i + d) % shares) for i in range(shares)])  16.1 us
    pallas_call x2, Pallas kernels, prep(): pl.pallas_call(functools.partial(prep_kernel, points, bins, blocks, group...  9.89 us
    unnamed x37, local copies, waits for them, and re-layouts  6.58 us
  transfers between devices with their start and end apart: 18, of which 3 were waited for; matrix products, arithmetic and copies ran while one was open for 3% of the time, Pallas kernels for 33%

profile of v3, /device:TPU:1, one launch (start us, length us, event | category | flops | bytes accessed | tf_op | source)
XLA Modules:
  0.0 189.6 jit_solution(2209792034053076306)
XLA Ops:
  0.0 3.1 %prep.2 = (f32[2,592,128]{2,1,0:T(8,128)}, f32[2,592,128]{2,1,0:T(8,128)}) custom-call(f32[324,4096]{1,0:T(8,128)} %spec_hbm.2, s32[1,4096]{1,0:T(1,128)} %bitcast.56), custom_call_target="tpu_custom_call" | custom-call | bytes 6000000 | tf_op jit(solution)/shard_map/prep/pallas_call | solution.py:300
  3.1 4.5 %collective-permute-start = (f32[2,592,128]{2,1,0:T(8,128)}, f32[2,592,128]{2,1,0:T(8,128)S(1)}, u32[]{:S(2)}, u32[]{:S(2)}) collective-permute-start(f32[2,592,128]{2,1,0:T(8,128)} %get-tuple-element.38), channel_id=1, source_target_pairs={{0,4},{4,8},{8,12},{1,5},{5,9},{9,13},{2,6},{6,10},{10,14},{3,7},{... | collective-permute-start | bytes 1818632 | tf_op jit(solution)/shard_map/ppermute | solution.py:611
  7.7 0.0 copy-start.14
  7.7 2.1 %collective-permute-start.1 = (f32[2,592,128]{2,1,0:T(8,128)}, f32[2,592,128]{2,1,0:T(8,128)S(1)}, u32[]{:S(2)}, u32[]{:S(2)}) collective-permute-start(f32[2,592,128]{2,1,0:T(8,128)} %get-tuple-element.39), channel_id=1, source_target_pairs={{4,0},{8,4},{12,8},{5,1},{9,5},{13,9},{6,2},{10,6},{14,10},{7,3},{... | collective-permute-start | bytes 1818632 | tf_op jit(solution)/shard_map/ppermute | solution.py:611
  9.8 6.8 %prep.3 = (f32[2,592,128]{2,1,0:T(8,128)}, f32[5,592,128]{2,1,0:T(8,128)}, f32[2,592,128]{2,1,0:T(8,128)}, f32[5,592,128]{2,1,0:T(8,128)}, f32[10368,128]{1,0:T(...) custom-call(f32[324,4096]{1,0:T(8,128)} %spec_hbm.2, s32[1,4096]{1,0:T(1,128)} %bitcast.57), custom_call_target="tpu_custom_call" | custom-call | bytes 27000000 | tf_op jit(solution)/shard_map/prep/pallas_call | solution.py:300
  16.5 3.2 %collective-permute-start.2 = (f32[1152,128]{1,0:T(8,128)}, f32[1152,128]{1,0:T(8,128)S(1)}, u32[]{:S(2)}, u32[]{:S(2)}) collective-permute-start(f32[1152,128]{1,0:T(8,128)} %get-tuple-element.42), channel_id=1, source_target_pairs={{0,1},{1,2},{2,3},{4,5},{5,6},{6,7},{8,9},{9,10},{10,11},{12,13},{... | collective-permute-start | bytes 1769480 | tf_op jit(solution)/shard_map/ppermute | solution.py:611
  19.8 1.3 collective-permute-start.3
  21.1 0.6 copy.21
  21.7 0.0 collective-permute-done.hs_ref
  21.7 0.0 collective-permute-done.1.hn_ref
  21.7 0.8 copy-done.3
  22.6 0.2 copy-done.4
  22.7 12.6 %front.4 = f32[4,72,8,128]{3,2,1,0:T(8,128)} custom-call(f32[36]{0:T(128)} %constant.21.clone.tab_ref, f32[2,36]{1,0:T(2,128)} %constant.24.clone.dir_ref, s32[1]{0:T(128)} %bitcast.2.pos_ref, s32[4,32,128]{2,1,0:T(8,128)} %bitcast.34, f32[32,128]{1,0:T(8,128)} %bitcast.40, f32[32,128]{1,0:T(8,128)} %bitcast.44, f32[32,128]{1,0:T(8,128)} %bitcast.48, ...), custom_call_target="tpu_custom_call" | custom-call | bytes 44000000 | tf_op jit(solution)/shard_map/front/pallas_call | solution.py:440
  35.4 5.4 %all-to-all-start = ((f32[4,72,8,128]{3,2,1,0:T(8,128)}), f32[4,72,8,128]{3,2,1,0:T(8,128)}, u32[]{:S(2)}, u32[]{:S(2)}) async-start(f32[4,72,8,128]{3,2,1,0:T(8,128)} %front.4), calls=%async_computation | async-start | bytes 2359296 | tf_op jit(solution)/shard_map/all_to_all | solution.py:645
  40.7 0.0 collective-permute-done.2
  40.7 0.0 collective-permute-done.3
  40.8 0.0 copy-start.6
  40.8 0.9 copy-done.5
  41.6 0.2 copy-done.6
  41.9 1.9 %collective-permute-start.10 = (f32[5,592,128]{2,1,0:T(8,128)}, f32[5,592,128]{2,1,0:T(8,128)S(1)}, u32[]{:S(2)}, u32[]{:S(2)}) collective-permute-start(f32[5,592,128]{2,1,0:T(8,128)} %get-tuple-element.55), channel_id=1, source_target_pairs={{4,0},{8,4},{12,8},{5,1},{9,5},{13,9},{6,2},{10,6},{14,10},{7,3},{... | collective-permute-start | bytes 4546568 | tf_op jit(solution)/shard_map/ppermute | solution.py:611
  43.8 4.5 %collective-permute-start.9 = (f32[5,592,128]{2,1,0:T(8,128)}, f32[5,592,128]{2,1,0:T(8,128)S(1)}, u32[]{:S(2)}, u32[]{:S(2)}) collective-permute-start(f32[5,592,128]{2,1,0:T(8,128)} %get-tuple-element.54), channel_id=1, source_target_pairs={{0,4},{4,8},{8,12},{1,5},{5,9},{9,13},{2,6},{6,10},{10,14},{3,7},{... | collective-permute-start | bytes 4546568 | tf_op jit(solution)/shard_map/ppermute | solution.py:611
  48.3 2.5 %collective-permute-start.4 = (f32[2,592,128]{2,1,0:T(8,128)}, f32[2,592,128]{2,1,0:T(8,128)}, u32[]{:S(2)}, u32[]{:S(2)}) collective-permute-start(f32[2,592,128]{2,1,0:T(8,128)} %get-tuple-element.45), channel_id=1, source_target_pairs={{0,4},{4,8},{8,12},{1,5},{5,9},{9,13},{2,6},{6,10},{10,14},{3,7},{... | collective-permute-start | bytes 1818632 | tf_op jit(solution)/shard_map/ppermute | solution.py:611
  50.8 2.6 %collective-permute-start.5 = (f32[2,592,128]{2,1,0:T(8,128)}, f32[2,592,128]{2,1,0:T(8,128)}, u32[]{:S(2)}, u32[]{:S(2)}) collective-permute-start(f32[2,592,128]{2,1,0:T(8,128)} %get-tuple-element.46), channel_id=1, source_target_pairs={{4,0},{8,4},{12,8},{5,1},{9,5},{13,9},{6,2},{10,6},{14,10},{7,3},{... | collective-permute-start | bytes 1818632 | tf_op jit(solution)/shard_map/ppermute | solution.py:611
  53.4 18.4 %collective-permute-done.4.hs_ref = f32[2,592,128]{2,1,0:T(8,128)} collective-permute-done((f32[2,592,128]{2,1,0:T(8,128)}, f32[2,592,128]{2,1,0:T(8,128)}, u32[]{:S(2)}, u32[]{:S(2)}) %collective-permute-start.4) | collective-permute-done | bytes 606240 | tf_op jit(solution)/shard_map/ppermute | solution.py:611
  71.8 0.0 collective-permute-done.5.hn_ref
  71.8 12.8 %front.5 = (f32[72,8,128]{2,1,0:T(8,128)}, f32[72,8,128]{2,1,0:T(8,128)}, f32[72,8,128]{2,1,0:T(8,128)}, f32[72,8,128]{2,1,0:T(8,128)}) custom-call(f32[36]{0:T(128)} %constant.21.clone.tab_ref, f32[2,36]{1,0:T(2,128)} %constant.24.clone.dir_ref, s32[1]{0:T(128)} %bitcast.2.pos_ref, s32[4,32,128]{2,1,0:T(8,128)} %bitcast.35, f32[32,128]{1,0:T(8,128)} %bitcast.41, ...), custom_call_target="tpu_custom_call" | custom-call | bytes 44000000 | tf_op jit(solution)/shard_map/front/pallas_call | solution.py:440
  84.6 1.8 collective-permute-start.6
  86.3 2.1 %collective-permute-start.7 = (f32[72,8,128]{2,1,0:T(8,128)}, f32[72,8,128]{2,1,0:T(8,128)}, u32[]{:S(2)}, u32[]{:S(2)}) collective-permute-start(f32[72,8,128]{2,1,0:T(8,128)} %get-tuple-element.49), channel_id=1, source_target_pairs={{0,2},{1,3},{2,0},{3,1},{4,6},{5,7},{6,4},{7,5},{8,10},{9,11},{10,... | collective-permute-start | bytes 884744 | tf_op jit(solution)/shard_map/ppermute | solution.py:653
  88.4 1.2 collective-permute-start.8
  89.6 0.0 all-to-all-done.refs_0_
  89.6 0.0 collective-permute-done.10.hn_ref
  89.6 0.0 collective-permute-done.9.hs_ref
  89.6 1.1 copy-done.1
  90.8 1.1 copy-done.2
  91.9 17.8 %front.6 = (f32[108,8,128]{2,1,0:T(8,128)}, f32[108,8,128]{2,1,0:T(8,128)}, f32[108,8,128]{2,1,0:T(8,128)}, f32[108,8,128]{2,1,0:T(8,128)}) custom-call(f32[36]{0:T(128)} %constant.21.clone.tab_ref, f32[2,36]{1,0:T(2,128)} %constant.24.clone.dir_ref, s32[1]{0:T(128)} %bitcast.2.pos_ref, s32[4,32,128]{2,1,0:T(8,128)} %bitcast.36, f32[32,128]{1,0:T(8,128)} %bitcast.42, ...), custom_call_target="tpu_custom_call" | custom-call | bytes 66000000 | tf_op jit(solution)/shard_map/front/pallas_call | solution.py:440
  109.7 0.0 collective-permute-done.6.refs_2_
  109.7 0.0 collective-permute-done.7.refs_3_
  109.7 0.0 collective-permute-done.8.refs_4_
  109.7 6.5 %collective-permute-start.13 = (f32[108,8,128]{2,1,0:T(8,128)}, f32[108,8,128]{2,1,0:T(8,128)S(1)}, u32[]{:S(2)}, u32[]{:S(2)}) collective-permute-start(f32[108,8,128]{2,1,0:T(8,128)} %get-tuple-element.62), channel_id=1, source_target_pairs={{0,3},{1,0},{2,1},{3,2},{4,7},{5,4},{6,5},{7,6},{8,11},{9,8},{10,9... | collective-permute-start | bytes 1327112 | tf_op jit(solution)/shard_map/ppermute | solution.py:653
  116.2 1.2 collective-permute-start.12
  117.4 0.0 collective-permute-start.11
  117.4 12.8 %front.7 = (f32[72,8,128]{2,1,0:T(8,128)}, f32[72,8,128]{2,1,0:T(8,128)}, f32[72,8,128]{2,1,0:T(8,128)}, f32[72,8,128]{2,1,0:T(8,128)}) custom-call(f32[36]{0:T(128)} %constant.21.clone.tab_ref, f32[2,36]{1,0:T(2,128)} %constant.24.clone.dir_ref, s32[1]{0:T(128)} %bitcast.2.pos_ref, s32[4,32,128]{2,1,0:T(8,128)} %bitcast.37, f32[32,128]{1,0:T(8,128)} %bitcast.43, ...), custom_call_target="tpu_custom_call" | custom-call | bytes 44000000 | tf_op jit(solution)/shard_map/front/pallas_call | solution.py:440
  130.3 0.0 collective-permute-done.13.refs_8_
  130.3 3.3 %collective-permute-start.16 = (f32[72,8,128]{2,1,0:T(8,128)}, f32[72,8,128]{2,1,0:T(8,128)S(1)}, u32[]{:S(2)}, u32[]{:S(2)}) collective-permute-start(f32[72,8,128]{2,1,0:T(8,128)} %get-tuple-element.70), channel_id=1, source_target_pairs={{0,3},{1,0},{2,1},{3,2},{4,7},{5,4},{6,5},{7,6},{8,11},{9,8},{10,9... | collective-permute-start | bytes 884744 | tf_op jit(solution)/shard_map/ppermute | solution.py:653
  133.6 22.1 %collective-permute-done.12.refs_7_ = f32[108,8,128]{2,1,0:T(8,128)S(1)} collective-permute-done((f32[108,8,128]{2,1,0:T(8,128)}, f32[108,8,128]{2,1,0:T(8,128)S(1)}, u32[]{:S(2)}, u32[]{:S(2)}) %collective-permute-start.12) | collective-permute-done | bytes 442400 | tf_op jit(solution)/shard_map/ppermute | solution.py:653
  155.7 0.0 collective-permute-start.15
  155.7 0.0 collective-permute-done.11.refs_6_
  155.7 0.1 collective-permute-start.14
  155.8 0.7 copy.22
  156.5 0.3 copy.15
  156.8 1.0 reshape.42.spot_ref
  157.7 0.0 copy-done.16
  157.7 0.3 copy.16
  158.0 0.9 reshape.43.wts_ref
  158.9 1.3 dynamic-slice_bitcast_fusion.1.mask_ref
  160.2 0.0 collective-permute-done.16.refs_12_
  160.2 5.3 %collective-permute-done.15.refs_11_ = f32[72,8,128]{2,1,0:T(8,128)S(1)} collective-permute-done((f32[72,8,128]{2,1,0:T(8,128)}, f32[72,8,128]{2,1,0:T(8,128)S(1)}, u32[]{:S(2)}, u32[]{:S(2)}) %collective-permute-start.15) | collective-permute-done | bytes 294944 | tf_op jit(solution)/shard_map/ppermute | solution.py:653
  165.6 0.0 collective-permute-done.14.refs_10_
  165.6 0.0 copy-done.8
  165.6 0.0 copy-done.9
  165.6 0.0 copy-done.11
  165.6 0.7 copy-done.12
  166.3 0.2 copy-done.13
  166.4 23.2 %tail.1 = f32[1296,1024]{1,0:T(8,128)} custom-call(s32[5184]{0:T(1024)} %reshape.42.spot_ref, f32[2592]{0:T(1024)} %reshape.43.wts_ref, f32[3,36]{1,0:T(4,128)} %constant.22.clone.ftab_ref, f32[1296]{0:T(1024)} %constant.23.clone.frs_ref, f32[2,36]{1,0:T(2,128)} %constant.24.clone.dir_ref, s32[1]{0:T(128)} %bitcast.2.pos_ref, f32[2,8,128]{2,1,0:T(8,128)} %bitcast.58, ...), custom_call_target="tpu_custom_call" | custom-call | bytes 70000000 | tf_op jit(solution)/shard_map/tail/pallas_call | solution.py:555
  (22 shorter events, 0.1 us)
Async XLA Ops:
  0.0 155.8 %copy-start = (f32[2,4096]{1,0:T(2,128)S(1)}, f32[2,4096]{1,0:T(2,128)}, u32[]{:S(2)}) copy-start(f32[2,4096]{1,0:T(2,128)} %param.15) | copy-start | bytes 98308
  3.1 18.6 %collective-permute-start = (f32[2,592,128]{2,1,0:T(8,128)}, f32[2,592,128]{2,1,0:T(8,128)S(1)}, u32[]{:S(2)}, u32[]{:S(2)}) collective-permute-start(f32[2,592,128]{2,1,0:T(8,128)} %get-tuple-element.38), channel_id=1, source_target_pairs={{0,4},{4,8},{8,12},{1,5},{5,9},{9,13},{2,6},{6,10},{10,14},{3,7},{... | collective-permute-start | bytes 1818632 | tf_op jit(solution)/shard_map/ppermute | solution.py:611
  7.7 13.4 %copy-start.14 = (s32[4,4096]{1,0:T(4,128)S(1)}, s32[4,4096]{1,0:T(4,128)}, u32[]{:S(2)}) copy-start(s32[4,4096]{1,0:T(4,128)} %param.17) | copy-start | bytes 196612
  7.7 14.0 %collective-permute-start.1 = (f32[2,592,128]{2,1,0:T(8,128)}, f32[2,592,128]{2,1,0:T(8,128)S(1)}, u32[]{:S(2)}, u32[]{:S(2)}) collective-permute-start(f32[2,592,128]{2,1,0:T(8,128)} %get-tuple-element.39), channel_id=1, source_target_pairs={{4,0},{8,4},{12,8},{5,1},{9,5},{13,9},{6,2},{10,6},{14,10},{7,3},{... | collective-permute-start | bytes 1818632 | tf_op jit(solution)/shard_map/ppermute | solution.py:611
  16.5 24.2 %collective-permute-start.2 = (f32[1152,128]{1,0:T(8,128)}, f32[1152,128]{1,0:T(8,128)S(1)}, u32[]{:S(2)}, u32[]{:S(2)}) collective-permute-start(f32[1152,128]{1,0:T(8,128)} %get-tuple-element.42), channel_id=1, source_target_pairs={{0,1},{1,2},{2,3},{4,5},{5,6},{6,7},{8,9},{9,10},{10,11},{12,13},{... | collective-permute-start | bytes 1769480 | tf_op jit(solution)/shard_map/ppermute | solution.py:611
  19.8 21.0 %collective-permute-start.3 = (f32[1152,128]{1,0:T(8,128)}, f32[1152,128]{1,0:T(8,128)S(1)}, u32[]{:S(2)}, u32[]{:S(2)}) collective-permute-start(f32[1152,128]{1,0:T(8,128)} %get-tuple-element.43), channel_id=1, source_target_pairs={{1,0},{2,1},{3,2},{5,4},{6,5},{7,6},{9,8},{10,9},{11,10},{13,12},{... | collective-permute-start | bytes 1769480 | tf_op jit(solution)/shard_map/ppermute | solution.py:611
  21.7 0.8 copy-start.3
  21.7 1.0 copy-start.4
  35.4 54.2 %all-to-all-start = ((f32[4,72,8,128]{3,2,1,0:T(8,128)}), f32[4,72,8,128]{3,2,1,0:T(8,128)}, u32[]{:S(2)}, u32[]{:S(2)}) async-start(f32[4,72,8,128]{3,2,1,0:T(8,128)} %front.4), calls=%async_computation | async-start | bytes 2359296 | tf_op jit(solution)/shard_map/all_to_all | solution.py:645
  40.7 0.9 copy-start.5
  40.8 1.1 copy-start.6
  41.9 47.8 %collective-permute-start.10 = (f32[5,592,128]{2,1,0:T(8,128)}, f32[5,592,128]{2,1,0:T(8,128)S(1)}, u32[]{:S(2)}, u32[]{:S(2)}) collective-permute-start(f32[5,592,128]{2,1,0:T(8,128)} %get-tuple-element.55), channel_id=1, source_target_pairs={{4,0},{8,4},{12,8},{5,1},{9,5},{13,9},{6,2},{10,6},{14,10},{7,3},{... | collective-permute-start | bytes 4546568 | tf_op jit(solution)/shard_map/ppermute | solution.py:611
  43.8 45.9 %collective-permute-start.9 = (f32[5,592,128]{2,1,0:T(8,128)}, f32[5,592,128]{2,1,0:T(8,128)S(1)}, u32[]{:S(2)}, u32[]{:S(2)}) collective-permute-start(f32[5,592,128]{2,1,0:T(8,128)} %get-tuple-element.54), channel_id=1, source_target_pairs={{0,4},{4,8},{8,12},{1,5},{5,9},{9,13},{2,6},{6,10},{10,14},{3,7},{... | collective-permute-start | bytes 4546568 | tf_op jit(solution)/shard_map/ppermute | solution.py:611
  48.3 23.5 %collective-permute-start.4 = (f32[2,592,128]{2,1,0:T(8,128)}, f32[2,592,128]{2,1,0:T(8,128)}, u32[]{:S(2)}, u32[]{:S(2)}) collective-permute-start(f32[2,592,128]{2,1,0:T(8,128)} %get-tuple-element.45), channel_id=1, source_target_pairs={{0,4},{4,8},{8,12},{1,5},{5,9},{9,13},{2,6},{6,10},{10,14},{3,7},{... | collective-permute-start | bytes 1818632 | tf_op jit(solution)/shard_map/ppermute | solution.py:611
  50.8 21.0 %collective-permute-start.5 = (f32[2,592,128]{2,1,0:T(8,128)}, f32[2,592,128]{2,1,0:T(8,128)}, u32[]{:S(2)}, u32[]{:S(2)}) collective-permute-start(f32[2,592,128]{2,1,0:T(8,128)} %get-tuple-element.46), channel_id=1, source_target_pairs={{4,0},{8,4},{12,8},{5,1},{9,5},{13,9},{6,2},{10,6},{14,10},{7,3},{... | collective-permute-start | bytes 1818632 | tf_op jit(solution)/shard_map/ppermute | solution.py:611
  84.6 25.2 %collective-permute-start.6 = (f32[72,8,128]{2,1,0:T(8,128)}, f32[72,8,128]{2,1,0:T(8,128)S(1)}, u32[]{:S(2)}, u32[]{:S(2)}) collective-permute-start(f32[72,8,128]{2,1,0:T(8,128)} %get-tuple-element.48), channel_id=1, source_target_pairs={{0,1},{1,2},{2,3},{3,0},{4,5},{5,6},{6,7},{7,4},{8,9},{9,10},{10,1... | collective-permute-start | bytes 884744 | tf_op jit(solution)/shard_map/ppermute | solution.py:653
  86.3 23.4 %collective-permute-start.7 = (f32[72,8,128]{2,1,0:T(8,128)}, f32[72,8,128]{2,1,0:T(8,128)}, u32[]{:S(2)}, u32[]{:S(2)}) collective-permute-start(f32[72,8,128]{2,1,0:T(8,128)} %get-tuple-element.49), channel_id=1, source_target_pairs={{0,2},{1,3},{2,0},{3,1},{4,6},{5,7},{6,4},{7,5},{8,10},{9,11},{10,... | collective-permute-start | bytes 884744 | tf_op jit(solution)/shard_map/ppermute | solution.py:653
  88.4 21.3 %collective-permute-start.8 = (f32[72,8,128]{2,1,0:T(8,128)}, f32[72,8,128]{2,1,0:T(8,128)}, u32[]{:S(2)}, u32[]{:S(2)}) collective-permute-start(f32[72,8,128]{2,1,0:T(8,128)} %get-tuple-element.50), channel_id=1, source_target_pairs={{0,3},{1,0},{2,1},{3,2},{4,7},{5,4},{6,5},{7,6},{8,11},{9,8},{10,9... | collective-permute-start | bytes 884744 | tf_op jit(solution)/shard_map/ppermute | solution.py:653
  89.6 1.1 copy-start.1
  90.8 1.2 copy-start.2
  109.7 20.5 %copy-start.10 = (f32[72,8,128]{2,1,0:T(8,128)}, f32[72,8,128]{2,1,0:T(8,128)S(1)}, u32[]{:S(2)}) copy-start(f32[72,8,128]{2,1,0:T(8,128)S(1)} %collective-permute-done.6.refs_2_) | copy-start | bytes 884740
  109.7 20.5 %collective-permute-start.13 = (f32[108,8,128]{2,1,0:T(8,128)}, f32[108,8,128]{2,1,0:T(8,128)S(1)}, u32[]{:S(2)}, u32[]{:S(2)}) collective-permute-start(f32[108,8,128]{2,1,0:T(8,128)} %get-tuple-element.62), channel_id=1, source_target_pairs={{0,3},{1,0},{2,1},{3,2},{4,7},{5,4},{6,5},{7,6},{8,11},{9,8},{10,9... | collective-permute-start | bytes 1327112 | tf_op jit(solution)/shard_map/ppermute | solution.py:653
  116.2 39.5 %collective-permute-start.12 = (f32[108,8,128]{2,1,0:T(8,128)}, f32[108,8,128]{2,1,0:T(8,128)S(1)}, u32[]{:S(2)}, u32[]{:S(2)}) collective-permute-start(f32[108,8,128]{2,1,0:T(8,128)} %get-tuple-element.60), channel_id=1, source_target_pairs={{0,2},{1,3},{2,0},{3,1},{4,6},{5,7},{6,4},{7,5},{8,10},{9,11},{10,... | collective-permute-start | bytes 1327112 | tf_op jit(solution)/shard_map/ppermute | solution.py:653
  117.4 38.3 %collective-permute-start.11 = (f32[108,8,128]{2,1,0:T(8,128)}, f32[108,8,128]{2,1,0:T(8,128)S(1)}, u32[]{:S(2)}, u32[]{:S(2)}) collective-permute-start(f32[108,8,128]{2,1,0:T(8,128)} %get-tuple-element.58), channel_id=1, source_target_pairs={{0,1},{1,2},{2,3},{3,0},{4,5},{5,6},{6,7},{7,4},{8,9},{9,10},{10,1... | collective-permute-start | bytes 1327112 | tf_op jit(solution)/shard_map/ppermute | solution.py:653
  117.4 39.1 %copy-start.15 = (s32[4,1296]{1,0:T(4,128)S(1)}, s32[4,1296]{1,0:T(4,128)}, u32[]{:S(2)}) copy-start(s32[4,1296]{1,0:T(4,128)} %param.22) | copy-start | bytes 62212
  117.4 40.3 %copy-start.16 = (f32[2,1296]{1,0:T(2,128)S(1)}, f32[2,1296]{1,0:T(2,128)}, u32[]{:S(2)}) copy-start(f32[2,1296]{1,0:T(2,128)} %param.23) | copy-start | bytes 31108
  130.3 35.3 %copy-start.7 = (f32[108,8,128]{2,1,0:T(8,128)}, f32[108,8,128]{2,1,0:T(8,128)S(1)}, u32[]{:S(2)}) copy-start(f32[108,8,128]{2,1,0:T(8,128)S(1)} %collective-permute-done.13.refs_8_) | copy-start | bytes 1327108
  130.3 30.0 %collective-permute-start.16 = (f32[72,8,128]{2,1,0:T(8,128)}, f32[72,8,128]{2,1,0:T(8,128)S(1)}, u32[]{:S(2)}, u32[]{:S(2)}) collective-permute-start(f32[72,8,128]{2,1,0:T(8,128)} %get-tuple-element.70), channel_id=1, source_target_pairs={{0,3},{1,0},{2,1},{3,2},{4,7},{5,4},{6,5},{7,6},{8,11},{9,8},{10,9... | collective-permute-start | bytes 884744 | tf_op jit(solution)/shard_map/ppermute | solution.py:653
  155.7 9.9 %copy-start.8 = (f32[108,8,128]{2,1,0:T(8,128)}, f32[108,8,128]{2,1,0:T(8,128)S(1)}, u32[]{:S(2)}) copy-start(f32[108,8,128]{2,1,0:T(8,128)S(1)} %collective-permute-done.12.refs_7_) | copy-start | bytes 1327108
  155.7 9.8 %collective-permute-start.15 = (f32[72,8,128]{2,1,0:T(8,128)}, f32[72,8,128]{2,1,0:T(8,128)S(1)}, u32[]{:S(2)}, u32[]{:S(2)}) collective-permute-start(f32[72,8,128]{2,1,0:T(8,128)} %get-tuple-element.68), channel_id=1, source_target_pairs={{0,2},{1,3},{2,0},{3,1},{4,6},{5,7},{6,4},{7,5},{8,10},{9,11},{10,... | collective-permute-start | bytes 884744 | tf_op jit(solution)/shard_map/ppermute | solution.py:653
  155.7 9.9 %copy-start.9 = (f32[108,8,128]{2,1,0:T(8,128)}, f32[108,8,128]{2,1,0:T(8,128)S(1)}, u32[]{:S(2)}) copy-start(f32[108,8,128]{2,1,0:T(8,128)S(1)} %collective-permute-done.11.refs_6_) | copy-start | bytes 1327108
  155.7 9.8 %collective-permute-start.14 = (f32[72,8,128]{2,1,0:T(8,128)}, f32[72,8,128]{2,1,0:T(8,128)S(1)}, u32[]{:S(2)}, u32[]{:S(2)}) collective-permute-start(f32[72,8,128]{2,1,0:T(8,128)} %get-tuple-element.66), channel_id=1, source_target_pairs={{0,1},{1,2},{2,3},{3,0},{4,5},{5,6},{6,7},{7,4},{8,9},{9,10},{10,1... | collective-permute-start | bytes 884744 | tf_op jit(solution)/shard_map/ppermute | solution.py:653
  160.2 5.4 %copy-start.11 = (f32[72,8,128]{2,1,0:T(8,128)}, f32[72,8,128]{2,1,0:T(8,128)S(1)}, u32[]{:S(2)}) copy-start(f32[72,8,128]{2,1,0:T(8,128)S(1)} %collective-permute-done.16.refs_12_) | copy-start | bytes 884740
  165.5 0.7 copy-start.12
  165.6 0.9 copy-start.13
